TPU v7x, 32 devices: a whole 2x2x4 slice. The times are simulated.
32 devices in a mesh: replica: 4 (over z), dp: 2 (over x), tensor: 4 (over y, core).
Axes of the slice: x: 2, y: 2, z: 4, core: 2. Of those that a mesh axis runs over, the one named last changes fastest.
Arguments:
- tokens: bfloat16 [4, 2048, 2048], P('replica', 'dp', 'tensor'), may hold values from -6 to 6
- grad_out: bfloat16 [4, 2048, 14336], P('replica', 'dp', 'tensor'), may hold values from -250 to 250, as said below
- weights: bfloat16 [4, 2048, 14336], P('replica', 'dp', 'tensor'), may hold values from -6 to 6
- first_moment: bfloat16 [4, 2048, 14336], P('replica', 'dp', 'tensor'), may hold values from -4 to 4
- second_moment: bfloat16 [4, 2048, 14336], P('replica', 'dp', 'tensor'), may hold values from 0.019897461 to 0.19921875
Outputs:
- new_weights: bfloat16 [4, 2048, 14336], P('replica', 'dp', 'tensor')
- new_first: bfloat16 [4, 2048, 14336], P('replica', 'dp', 'tensor')
- new_second: bfloat16 [4, 2048, 14336], P('replica', 'dp', 'tensor')
Inputs may be any that keep to these rules, and one draw needn't show every extreme that they name: `grad_out`: the upstream gradient.
All inputs are finite; a program needn't handle non-finite values.
Results may differ from a plain program's by a relative error of at most 0.0051.
Values may be sent and summed in bfloat16 or wider, within the bound.
A program may use at most 192 MiB of HBM per device.

v0:
```python
import jax
import jax.numpy as jnp
from jax import lax
from jax.sharding import PartitionSpec as P

D = 2048
FF = 14336
STEP = 1


def partner(value, axis, bit):
    mask = 2**bit
    pairs = [(source, source ^ mask) for source in range(lax.axis_size(axis))]
    return lax.ppermute(value, axis, pairs)


def adamw(grad, total, weights, first_moment, second_moment):
    clip = jnp.minimum(1.0, 1.0 / jnp.sqrt(total / (D * FF) + 1e-06))
    scaled = clip * grad
    moment_one = 0.9 * first_moment.astype(jnp.float32) + 0.1 * scaled
    moment_two = 0.95 * second_moment.astype(jnp.float32) + 0.05 * scaled * scaled
    fix_one = 1.0 - 0.9**STEP
    fix_two = 1.0 - 0.95**STEP
    update = moment_one / fix_one / (jnp.sqrt(moment_two / fix_two) + 1e-08)
    old = weights.astype(jnp.float32)
    fresh = old - 0.05 * (update + 0.1 * old)
    return jnp.stack(
        [
            fresh.astype(jnp.bfloat16),
            moment_one.astype(jnp.bfloat16),
            moment_two.astype(jnp.bfloat16),
        ]
    )


def body(tokens, grad_out, weights, first_moment, second_moment):
    whole = lax.all_gather(tokens[0], "tensor", axis=1, tiled=True)
    upstream = grad_out[0]
    grad = lax.psum_scatter(
        lax.dot_general(
            whole, upstream, (((0,), (0,)), ((), ())), preferred_element_type=jnp.float32
        ),
        "dp",
        scatter_dimension=0,
        tiled=True,
    )
    local_sq = jnp.sum(grad * grad)
    bit_index = lax.axis_size("replica").bit_length() - 2
    total = lax.psum(local_sq, ("dp", "tensor"))
    states = adamw(grad, total, weights[0], first_moment[0], second_moment[0])
    others = partner(states, "replica", bit_index)
    mixed = (0.5 * (states.astype(jnp.float32) + others.astype(jnp.float32))).astype(jnp.bfloat16)
    return (mixed[0][None], mixed[1][None], mixed[2][None])


def solution(mesh):
    placed = (
        P("replica", "dp", "tensor"),
        P("replica", "dp", "tensor"),
        P("replica", "dp", "tensor"),
        P("replica", "dp", "tensor"),
        P("replica", "dp", "tensor"),
    )
    return jax.shard_map(
        body,
        mesh=mesh,
        in_specs=placed,
        out_specs=(
            P("replica", "dp", "tensor"),
            P("replica", "dp", "tensor"),
            P("replica", "dp", "tensor"),
        ),
        check_vma=False,
    )
```

profile of v0, /device:TPU:0, one launch (start us, length us, event | category | flops | bytes accessed | tf_op | source)
XLA Modules:
  0.0 1445.3 jit_solution(11597820317019363386)
XLA Ops:
  7.2 0.0 all-gather.3.cloned.1.call-start
  7.2 0.7 all-gather.3.cloned.1.call-update
  7.9 0.0 reduce-scatter.2.cloned.1.call-start
  7.9 38.8 %all-gather.3.cloned.1.call-done = bf16[1,1024,2048]{2,1,0:T(8,128)(2,1)} async-done(((bf16[1,1024,512]{2,1,0:T(8,128)(2,1)}), bf16[1,1024,2048]{2,1,0:T(8,128)(2,1)}) %all-gather.3.cloned.1.call-update) | async-done | bytes 4194320 | tf_op jit(solution)/shard_map/all_gather | solution.py:37
  46.8 24.3 %fusion.6 = f32[2048,3584]{1,0:T(8,128)} fusion(bf16[1,1024,3584]{2,1,0:T(8,128)(2,1)} %param.6, bf16[1,1024,2048]{2,1,0:T(8,128)(2,1)} %all-gather.3.cloned.1.call-done), kind=kOutput, calls=%fused_computation.13 | convolution fusion | flops 15032385536 | bytes 40894464 | tf_op jit(solution)/shard_map/dot_general | solution.py:40
  71.1 0.0 reduce-scatter.2.cloned.1.call-update
  71.1 324.5 %reduce-scatter.2.cloned.1.call-done = f32[1024,3584]{1,0:T(8,128)} async-done(((f32[2048,3584]{1,0:T(8,128)}), f32[1024,3584]{1,0:T(8,128)}) %reduce-scatter.2.cloned.1.call-update) | async-done | bytes 14680080 | tf_op jit(solution)/shard_map/reduce_scatter | solution.py:39
  395.7 9.5 multiply_reduce_fusion
  405.2 13.5 psum.7
  419.4 18.3 %fusion.8 = (bf16[1,1024,3584]{2,1,0:T(8,128)(2,1)S(1)}, bf16[1,1024,3584]{2,1,0:T(8,128)(2,1)S(1)}, bf16[1,1024,3584]{2,1,0:T(8,128)(2,1)S(1)}) fusion(bf16[1,1024,3584]{2,1,0:T(8,128)(2,1)} %param.9, f32[1024,3584]{1,0:T(8,128)} %reduce-scatter.2.cloned.1.call-done, f32[]{:T(128)S(6)} %min.3, bf16[1,1024,3584]{2,1,0:T(8,128)(2,1)} %param.8, ...), kind=kLoop, calls=%fused_computation.16 | loop fusion | flops 80740352 | bytes 58720260 | tf_op jit(solution)/shard_map/stack | solution.py:27
  437.7 0.0 copy-start
  437.7 0.0 copy-start.1
  437.7 0.0 copy-start.2
  437.7 14.1 pad_maximum_fusion
  451.8 0.0 copy-done
  451.8 0.0 copy-done.1
  451.8 0.0 copy-done.2
  451.8 2.5 collective-permute-start
  454.3 944.1 %collective-permute-done = bf16[3,1024,3584]{2,1,0:T(8,128)(2,1)} collective-permute-done((bf16[3,1024,3584]{2,1,0:T(8,128)(2,1)}, bf16[3,1024,3584]{2,1,0:T(8,128)(2,1)}, u32[]{:S(2)}, u32[]{:S(2)}) %collective-permute-start) | collective-permute-done | bytes 22020128 | tf_op jit(solution)/shard_map/ppermute | solution.py:14
  1398.4 25.6 %multiply_convert_fusion = bf16[3,1024,3584]{2,1,0:T(8,128)(2,1)} fusion(bf16[3,1024,3584]{2,1,0:T(8,128)(2,1)} %collective-permute-done, bf16[1,1024,3584]{2,1,0:T(8,128)(2,1)} %copy-done.2, bf16[1,1024,3584]{2,1,0:T(8,128)(2,1)} %copy-done.1, bf16[1,1024,3584]{2,1,0:T(8,128)(2,1)} %copy-done), kind=kLoop, calls=%fused_computation | loop fusion | flops 77070336 | bytes 66060288 | tf_op jit(solution)/shard_map/convert_element_type | solution.py:52
  1424.0 14.4 fusion.10
Async XLA Ops:
  7.2 39.6 %all-gather.3.cloned.1.call-start = ((), (), s32[]{:S(2)}) async-start(), calls=%async_computation.2 | async-start | bytes 5242880 | tf_op jit(solution)/shard_map/all_gather | solution.py:37
  7.9 387.8 %reduce-scatter.2.cloned.1.call-start = ((), (), s32[]{:S(2)}) async-start(), calls=%async_computation.1 | async-start | bytes 44040192 | tf_op jit(solution)/shard_map/reduce_scatter | solution.py:39
  437.7 14.1 copy-start
  437.7 14.1 copy-start.1
  437.7 14.1 copy-start.2
  451.8 946.6 %collective-permute-start = (bf16[3,1024,3584]{2,1,0:T(8,128)(2,1)}, bf16[3,1024,3584]{2,1,0:T(8,128)(2,1)}, u32[]{:S(2)}, u32[]{:S(2)}) collective-permute-start(bf16[3,1024,3584]{2,1,0:T(8,128)(2,1)} %pad_maximum_fusion), channel_id=1, source_target_pairs={{0,16},{8,24},{16,0},{24,8},{1,17},{9,25},{17,1},{25,9},{2,18},{10... | collective-permute-start | bytes 66060296 | tf_op jit(solution)/shard_map/ppermute | solution.py:14
Sparse Core Ops, SparseCore 0:
  9.6 37.1 all-gather.2
  71.2 324.3 reduce-scatter.1
where the time goes:
time: 1450 us
  waiting for transfers between devices  1310 us (90%)
  other arithmetic  67.5 us (5%)
  matrix products  24.3 us (2%)
  between operations  14.8 us (1%)
    ppermute x1, waiting for transfers between devices, partner(): return lax.ppermute(value, axis, pairs)  944 us
    reduce_scatter x1, waiting for transfers between devices, body(): lax.psum_scatter(lax.dot_general(whole, upstream, (((0,), (0,)), ((), ())...  325 us
    all_gather x1, waiting for transfers between devices, body(): whole = lax.all_gather(tokens[0], 'tensor', axis=1, tiled=True)  38.8 us
    another operation x2, other arithmetic, adamw(): jnp.stack([fresh.astype(jnp.bfloat16), moment_one.astype(jnp.bfloat16), m...  32.4 us
  transfers between devices with their start and end apart: 3, of which 3 were waited for; matrix products, arithmetic and copies ran while one was open for 0% of the time, Pallas kernels for 0%

commit v1 on v0

v1 whole, which is shorter than its diff:
```python
import functools

import jax
import jax.numpy as jnp
from jax import lax
from jax.experimental import pallas as pl
from jax.experimental.pallas import tpu as pltpu
from jax.sharding import PartitionSpec as P

D = 2048
FF = 14336
STEP = 1
FIX_ONE = 1.0 - 0.9**STEP
FIX_TWO = 1.0 - 0.95**STEP
TILE = 32
SHARES = (8, 5, 2, 1)


def partner(value, axis, bit):
    mask = 2**bit
    pairs = [(source, source ^ mask) for source in range(lax.axis_size(axis))]
    return lax.ppermute(value, axis, pairs)


def second_kernel(clip_ref, grad_ref, second_ref, after_ref, out_ref):
    scaled = clip_ref[0, 0] * grad_ref[...]
    fresh = 0.95 * second_ref[...].astype(jnp.float32) + 0.05 * scaled * scaled
    out_ref[...] = fresh.astype(jnp.bfloat16)


def second_chunk(clip, grad, second, after, start, rows):
    cols = grad.shape[1]
    first = start // TILE
    return pl.pallas_call(
        second_kernel,
        grid=(rows // TILE,),
        in_specs=[
            pl.BlockSpec(memory_space=pltpu.SMEM),
            pl.BlockSpec((TILE, cols), lambda i: (first + i, 0)),
            pl.BlockSpec((TILE, cols), lambda i: (first + i, 0)),
            pl.BlockSpec(memory_space=pl.ANY),
        ],
        out_specs=pl.BlockSpec((TILE, cols), lambda i: (i, 0)),
        out_shape=jax.ShapeDtypeStruct((rows, cols), jnp.bfloat16),
        cost_estimate=pl.CostEstimate(
            flops=6 * rows * cols, bytes_accessed=8 * rows * cols, transcendentals=0
        ),
        compiler_params=pltpu.CompilerParams(vmem_limit_bytes=60 * 2**20),
    )(clip, grad, second, after)


def new_weights(old, first, second):
    old = old.astype(jnp.float32)
    first = first.astype(jnp.float32)
    second = second.astype(jnp.float32)
    update = first / FIX_ONE / (jnp.sqrt(second / FIX_TWO) + 1e-08)
    fresh = old - 0.05 * (update + 0.1 * old)
    return fresh.astype(jnp.bfloat16)


def mean(one, two):
    return (0.5 * (one.astype(jnp.float32) + two.astype(jnp.float32))).astype(jnp.bfloat16)


def mix_kernel(w, w2, m, m2, v, v2, *refs):
    out_w, out_m, out_v = refs[-3:]
    first, first2 = m[...], m2[...]
    second, second2 = v[...], v2[...]
    out_m[...] = mean(first, first2)
    out_v[...] = mean(second, second2)
    out_w[...] = mean(
        new_weights(w[...], first, second), new_weights(w2[...], first2, second2)
    )


def mix_chunk(w, w2, m, m2, v, v2, held, start):
    rows, cols = v.shape
    first = start // TILE
    far = pl.BlockSpec((TILE, cols), lambda i: (first + i, 0))
    near = pl.BlockSpec((TILE, cols), lambda i: (i, 0))
    held = tuple(held)
    return pl.pallas_call(
        mix_kernel,
        grid=(rows // TILE,),
        in_specs=[far, far, far, far, near, near] + [pl.BlockSpec(memory_space=pl.ANY)] * len(held),
        out_specs=(far, far, far),
        out_shape=(jax.ShapeDtypeStruct(w.shape, jnp.bfloat16),) * 3,
        input_output_aliases={6 + i: i for i in range(len(held))},
        cost_estimate=pl.CostEstimate(
            flops=30 * rows * cols, bytes_accessed=18 * rows * cols, transcendentals=4 * rows * cols
        ),
        compiler_params=pltpu.CompilerParams(vmem_limit_bytes=60 * 2**20),
    )(w, w2, m, m2, v, v2, *held)


def contract(one, two):
    return lax.dot_general(one, two, (((0,), (0,)), ((), ())), preferred_element_type=jnp.float32)


def body(tokens, grad_out, weights, first_moment, second_moment):
    bit = lax.axis_size("replica").bit_length() - 2
    weights, upstream = weights[0], grad_out[0]
    first_moment, second_moment = first_moment[0], second_moment[0]
    rows = weights.shape[0]

    weights2 = partner(weights, "replica", bit)
    upstream2 = partner(upstream, "dp", 0)
    here = lax.axis_index("dp")
    whole = lax.all_gather(tokens[0], "tensor", axis=1, tiled=True)
    mine = lax.dynamic_slice_in_dim(whole, here * rows, rows, 1)
    theirs = lax.dynamic_slice_in_dim(whole, (1 - here) * rows, rows, 1)
    mine2 = partner(theirs, "dp", 0)
    grad = contract(mine, upstream) + contract(mine2, upstream2)
    total = lax.psum(jnp.sum(grad * grad), ("dp", "tensor"))
    clip = jnp.minimum(1.0, 1.0 / jnp.sqrt(total / (D * FF) + 1e-06))
    first = (0.9 * first_moment.astype(jnp.float32) + 0.1 * (clip * grad)).astype(jnp.bfloat16)
    first2 = partner(first, "replica", bit)

    clip = clip.reshape(1, 1)
    arrived = [weights2, first2]
    start, chunks = 0, []
    for share in SHARES:
        size = rows * share // sum(SHARES)
        second = second_chunk(clip, grad, second_moment, arrived[-2], start, size)
        second2 = partner(second, "replica", bit)
        arrived.append(second2)
        chunks.append((start, second, second2))
        start += size
    outs = ()
    for start, second, second2 in chunks:
        outs = mix_chunk(weights, weights2, first, first2, second, second2, outs, start)
    return tuple(out[None] for out in outs)


def solution(mesh):
    placed = P("replica", "dp", "tensor")
    return jax.shard_map(
        body,
        mesh=mesh,
        in_specs=(placed,) * 5,
        out_specs=(placed,) * 3,
        check_vma=False,
    )
```

time: 1450 us -> 1020 us (0.70)
  waiting for transfers between devices: 1310 us -> 863 us
  Pallas kernels: 0 us -> 70.5 us
  other arithmetic: 67.5 us -> 10.7 us
    reduce_scatter x1 -> x0, waiting for transfers between devices: 325 us -> none  [body(): lax.psum_scatter(lax.dot_general(whole, upstream, (((0,), (0,)), ((), ())...]
    ppermute x1 -> x8, waiting for transfers between devices: 944 us -> 826 us  [partner(): return lax.ppermute(value, axis, pairs)]
    pallas_call x0 -> x8, Pallas kernels: none -> 70.5 us  [the longest x4 45 us: mix_chunk(): pl.pallas_call(mix_kernel, grid=(rows // TILE,), in_specs=[far, far, far,...]
    another operation x2 -> x0, other arithmetic: 32.4 us -> none  [adamw(): jnp.stack([fresh.astype(jnp.bfloat16), moment_one.astype(jnp.bfloat16), m...]
    convert_element_type x1, other arithmetic: 25.6 us -> 10.7 us  [body(): (0.9 * first_moment.astype(jnp.float32) + 0.1 * (clip * grad)).astype(jnp...]
  transfers between devices with their start and end apart: 3 -> 9, of which waited for: 3 -> 7; matrix products, arithmetic and copies ran while one was open for 0% -> 4% of each run, Pallas kernels for 0% -> 7%
where the time goes in v1:
time: 1020 us
  waiting for transfers between devices  863 us (85%)
  Pallas kernels  70.5 us (7%)
  matrix products  27.2 us (3%)
  between operations  14.8 us (1%)
  blocking collectives  14.6 us (1%)
  other arithmetic  10.7 us (1%)
    ppermute x8, waiting for transfers between devices, partner(): return lax.ppermute(value, axis, pairs)  826 us
    pallas_call x4, Pallas kernels, mix_chunk(): pl.pallas_call(mix_kernel, grid=(rows // TILE,), in_specs=[far, far, far,...  45 us
    all_gather x1, waiting for transfers between devices, body(): whole = lax.all_gather(tokens[0], 'tensor', axis=1, tiled=True)  35.9 us
    dot_general x2, matrix products, contract(): lax.dot_general(one, two, (((0,), (0,)), ((), ())), preferred_element_typ...  27.2 us
    pallas_call x4, Pallas kernels, second_chunk(): pl.pallas_call(second_kernel, grid=(rows // TILE,), in_specs=[pl.BlockSpe...  25.5 us
  transfers between devices with their start and end apart: 9, of which 7 were waited for; matrix products, arithmetic and copies ran while one was open for 4% of the time, Pallas kernels for 7%

profile of v1, /device:TPU:0, one launch (start us, length us, event | category | flops | bytes accessed | tf_op | source)
XLA Modules:
  0.0 1016.3 jit_solution(8507271777407260856)
XLA Ops:
  7.2 0.0 all-gather.3.cloned.1.call-start
  7.2 0.7 all-gather.3.cloned.1.call-update
  7.9 3.0 collective-permute-start.2
  10.9 35.9 %all-gather.3.cloned.1.call-done = bf16[1,1024,2048]{2,1,0:T(8,128)(2,1)} async-done(((bf16[1,1024,512]{2,1,0:T(8,128)(2,1)}), bf16[1,1024,2048]{2,1,0:T(8,128)(2,1)}) %all-gather.3.cloned.1.call-update) | async-done | bytes 4194320 | tf_op jit(solution)/shard_map/all_gather | solution.py:109
  46.8 3.1 dynamic-slice_bitcast_fusion
  49.9 1.5 collective-permute-start.1
  51.3 2.4 collective-permute-start
  53.7 11.1 %fusion.1 = f32[1024,3584]{1,0:T(8,128)S(1)} fusion(bf16[1,1024,2048]{2,1,0:T(8,128)(2,1)} %all-gather.3.cloned.1.call-done, s32[]{:T(128)S(6)} %select_n.6, bf16[1,1024,3584]{2,1,0:T(8,128)(2,1)} %param.6), kind=kOutput, calls=%fused_computation.4 | convolution fusion | flops 7516192768 | bytes 24117252 | tf_op jit(solution)/shard_map/dot_general | solution.py:97
  64.9 105.1 %collective-permute-done.2 = bf16[1024,3584]{1,0:T(8,128)(2,1)} collective-permute-done((bf16[1024,3584]{1,0:T(8,128)(2,1)}, bf16[1024,3584]{1,0:T(8,128)(2,1)}, u32[]{:S(2)}, u32[]{:S(2)}) %collective-permute-start.2) | collective-permute-done | bytes 7340064 | tf_op jit(solution)/shard_map/ppermute | solution.py:22
  170.0 44.1 %collective-permute-done.1 = bf16[1024,1024]{1,0:T(8,128)(2,1)} collective-permute-done((bf16[1024,1024]{1,0:T(8,128)(2,1)}, bf16[1024,1024]{1,0:T(8,128)(2,1)}, u32[]{:S(2)}, u32[]{:S(2)}) %collective-permute-start.1) | collective-permute-done | bytes 2097184 | tf_op jit(solution)/shard_map/ppermute | solution.py:22
  214.1 16.0 %multiply_reduce_fusion = (f32[]{:T(128)}, f32[1024,3584]{1,0:T(8,128)}) fusion(f32[1024,3584]{1,0:T(8,128)S(1)} %fusion.1, bf16[1024,1024]{1,0:T(8,128)(2,1)} %collective-permute-done.1, bf16[1024,3584]{1,0:T(8,128)(2,1)} %collective-permute-done.2), kind=kOutput, calls=%fused_computation.2 | convolution fusion | flops 7527202816 | bytes 38797316 | tf_op jit(solution)/shard_map/dot_general | solution.py:97
  230.2 14.6 %psum.7 = f32[]{:T(128)} all-reduce(f32[]{:T(128)} %get-tuple-element.27), channel_id=1, replica_groups=mesh['replica'=4,'dp'=2,'tensor'=4] {'dp','tensor'}, use_global_device_ids=true, to_apply=%region_1.0 | all-reduce | flops 1 | bytes 8 | tf_op jit(solution)/shard_map/psum | solution.py:114
  245.5 10.7 %fusion.m = bf16[1024,3584]{1,0:T(8,128)(2,1)} fusion(f32[1024,3584]{1,0:T(8,128)} %get-tuple-element.28.grad_ref, bf16[1,1024,3584]{2,1,0:T(8,128)(2,1)} %param.8, f32[]{:T(128)} %min.3), kind=kLoop, calls=%fused_computation.1 | loop fusion | flops 22020096 | bytes 29360132 | tf_op jit(solution)/shard_map/convert_element_type | solution.py:116
  256.2 1.8 collective-permute-start.3
  258.0 269.9 %collective-permute-done.after_ref.w2 = bf16[1024,3584]{1,0:T(8,128)(2,1)} collective-permute-done((bf16[1024,3584]{1,0:T(8,128)(2,1)}, bf16[1024,3584]{1,0:T(8,128)(2,1)}, u32[]{:S(2)}, u32[]{:S(2)}) %collective-permute-start) | collective-permute-done | bytes 7340064 | tf_op jit(solution)/shard_map/ppermute | solution.py:22
  528.0 11.8 %shard_map.78.v = bf16[512,3584]{1,0:T(8,128)(2,1)} custom-call(f32[1,1]{1,0:T(1,128)} %bitcast.5.clip_ref, f32[1024,3584]{1,0:T(8,128)} %get-tuple-element.28.grad_ref, bf16[1024,3584]{1,0:T(8,128)(2,1)} %bitcast.20, bf16[1024,3584]{1,0:T(8,128)(2,1)} %collective-permute-done.after_ref.w2), custom_call_target="tpu_custom_call" | custom-call | flops 11010048 | bytes 14680064 | tf_op jit(solution)/shard_map/pallas_call | solution.py:34
  539.8 0.0 collective-permute-start.6
  539.8 224.1 %collective-permute-done.3.after_ref.m2 = bf16[1024,3584]{1,0:T(8,128)(2,1)} collective-permute-done((bf16[1024,3584]{1,0:T(8,128)(2,1)}, bf16[1024,3584]{1,0:T(8,128)(2,1)}, u32[]{:S(2)}, u32[]{:S(2)}) %collective-permute-start.3) | collective-permute-done | bytes 7340064 | tf_op jit(solution)/shard_map/ppermute | solution.py:22
  763.9 7.8 shard_map.76.v
  771.8 0.0 collective-permute-start.4
  771.8 119.9 %collective-permute-done.6.after_ref.v2 = bf16[512,3584]{1,0:T(8,128)(2,1)S(1)} collective-permute-done((bf16[512,3584]{1,0:T(8,128)(2,1)}, bf16[512,3584]{1,0:T(8,128)(2,1)S(1)}, u32[]{:S(2)}, u32[]{:S(2)}) %collective-permute-start.6) | collective-permute-done | bytes 3670048 | tf_op jit(solution)/shard_map/ppermute | solution.py:22
  891.6 0.0 copy-start
  891.6 1.8 copy-done
  893.5 3.8 shard_map.79.v
  897.3 0.0 collective-permute-start.7
  897.3 63.3 %collective-permute-done.4.after_ref.v2 = bf16[320,3584]{1,0:T(8,128)(2,1)} collective-permute-done((bf16[320,3584]{1,0:T(8,128)(2,1)}, bf16[320,3584]{1,0:T(8,128)(2,1)}, u32[]{:S(2)}, u32[]{:S(2)}) %collective-permute-start.4) | collective-permute-done | bytes 2293792 | tf_op jit(solution)/shard_map/ppermute | solution.py:22
  960.5 2.1 shard_map.77.v
  962.6 0.0 collective-permute-start.5
  962.6 21.2 %shard_map.80 = (bf16[1024,3584]{1,0:T(8,128)(2,1)}, bf16[1024,3584]{1,0:T(8,128)(2,1)}, bf16[1024,3584]{1,0:T(8,128)(2,1)}) custom-call(bf16[1024,3584]{1,0:T(8,128)(2,1)} %bitcast.25, bf16[1024,3584]{1,0:T(8,128)(2,1)} %collective-permute-done.after_ref.w2, bf16[1024,3584]{1,0:T(8,128)(2,1)} %fusion.m, ...), custom_call_target="tpu_custom_call" | custom-call | flops 55050240 | bytes 33030144 | tf_op jit(solution)/shard_map/pallas_call | solution.py:82
  983.8 13.8 %shard_map.81 = (bf16[1024,3584]{1,0:T(8,128)(2,1)}, bf16[1024,3584]{1,0:T(8,128)(2,1)}, bf16[1024,3584]{1,0:T(8,128)(2,1)}) custom-call(bf16[1024,3584]{1,0:T(8,128)(2,1)} %bitcast.26, bf16[1024,3584]{1,0:T(8,128)(2,1)} %collective-permute-done.after_ref.w2, bf16[1024,3584]{1,0:T(8,128)(2,1)} %fusion.m, ...), custom_call_target="tpu_custom_call", output_to_operand_aliasing={{0}: (6, {}), {1}: (7, {}), {2}: (8, {})} | custom-call | flops 34406400 | bytes 20643840 | tf_op jit(solution)/shard_map/pallas_call | solution.py:82
  997.6 0.0 collective-permute-done.7.v2
  997.6 0.0 copy-start.1
  997.6 1.0 copy-done.1
  998.6 6.3 shard_map.82
  1004.9 0.0 collective-permute-done.5.v2
  1004.9 0.0 copy-start.2
  1004.9 0.8 copy-done.2
  1005.6 3.8 shard_map.83
Async XLA Ops:
  7.2 39.6 %all-gather.3.cloned.1.call-start = ((), (), s32[]{:S(2)}) async-start(), calls=%async_computation | async-start | bytes 5242880 | tf_op jit(solution)/shard_map/all_gather | solution.py:109
  7.9 162.1 %collective-permute-start.2 = (bf16[1024,3584]{1,0:T(8,128)(2,1)}, bf16[1024,3584]{1,0:T(8,128)(2,1)}, u32[]{:S(2)}, u32[]{:S(2)}) collective-permute-start(bf16[1024,3584]{1,0:T(8,128)(2,1)} %bitcast.32), channel_id=1, source_target_pairs={{0,4},{4,0},{1,5},{5,1},{2,6},{6,2},{3,7},{7,3},{8,12},{12,8},{9,1... | collective-permute-start | bytes 22020104 | tf_op jit(solution)/shard_map/ppermute | solution.py:22
  49.9 164.3 %collective-permute-start.1 = (bf16[1024,1024]{1,0:T(8,128)(2,1)}, bf16[1024,1024]{1,0:T(8,128)(2,1)}, u32[]{:S(2)}, u32[]{:S(2)}) collective-permute-start(bf16[1024,1024]{1,0:T(8,128)(2,1)} %dynamic-slice_bitcast_fusion), channel_id=1, source_target_pairs={{0,4},{4,0},{1,5},{5,1},{2,6},{6,2},{3,7},{7,3},{8,12},{12,8},{9,1... | collective-permute-start | bytes 6291464 | tf_op jit(solution)/shard_map/ppermute | solution.py:22
  51.3 476.6 %collective-permute-start = (bf16[1024,3584]{1,0:T(8,128)(2,1)}, bf16[1024,3584]{1,0:T(8,128)(2,1)}, u32[]{:S(2)}, u32[]{:S(2)}) collective-permute-start(bf16[1024,3584]{1,0:T(8,128)(2,1)} %bitcast.24), channel_id=1, source_target_pairs={{0,16},{8,24},{16,0},{24,8},{1,17},{9,25},{17,1},{25,9},{2,18},{10... | collective-permute-start | bytes 22020104 | tf_op jit(solution)/shard_map/ppermute | solution.py:22
  256.2 507.7 %collective-permute-start.3 = (bf16[1024,3584]{1,0:T(8,128)(2,1)}, bf16[1024,3584]{1,0:T(8,128)(2,1)}, u32[]{:S(2)}, u32[]{:S(2)}) collective-permute-start(bf16[1024,3584]{1,0:T(8,128)(2,1)} %fusion.m), channel_id=1, source_target_pairs={{0,16},{8,24},{16,0},{24,8},{1,17},{9,25},{17,1},{25,9},{2,18},{10... | collective-permute-start | bytes 22020104 | tf_op jit(solution)/shard_map/ppermute | solution.py:22
  539.8 351.8 %collective-permute-start.6 = (bf16[512,3584]{1,0:T(8,128)(2,1)}, bf16[512,3584]{1,0:T(8,128)(2,1)S(1)}, u32[]{:S(2)}, u32[]{:S(2)}) collective-permute-start(bf16[512,3584]{1,0:T(8,128)(2,1)} %shard_map.78.v), channel_id=1, source_target_pairs={{0,16},{8,24},{16,0},{24,8},{1,17},{9,25},{17,1},{25,9},{2,18},{10... | collective-permute-start | bytes 11010056 | tf_op jit(solution)/shard_map/ppermute | solution.py:22
  771.8 188.8 %collective-permute-start.4 = (bf16[320,3584]{1,0:T(8,128)(2,1)}, bf16[320,3584]{1,0:T(8,128)(2,1)}, u32[]{:S(2)}, u32[]{:S(2)}) collective-permute-start(bf16[320,3584]{1,0:T(8,128)(2,1)} %shard_map.76.v), channel_id=1, source_target_pairs={{0,16},{8,24},{16,0},{24,8},{1,17},{9,25},{17,1},{25,9},{2,18},{10... | collective-permute-start | bytes 6881288 | tf_op jit(solution)/shard_map/ppermute | solution.py:22
  891.6 1.8 copy-start
  897.3 100.3 %collective-permute-start.7 = (bf16[128,3584]{1,0:T(8,128)(2,1)}, bf16[128,3584]{1,0:T(8,128)(2,1)S(1)}, u32[]{:S(2)}, u32[]{:S(2)}) collective-permute-start(bf16[128,3584]{1,0:T(8,128)(2,1)} %shard_map.79.v), channel_id=1, source_target_pairs={{0,16},{8,24},{16,0},{24,8},{1,17},{9,25},{17,1},{25,9},{2,18},{10... | collective-permute-start | bytes 2752520 | tf_op jit(solution)/shard_map/ppermute | solution.py:22
  962.6 42.2 %collective-permute-start.5 = (bf16[64,3584]{1,0:T(8,128)(2,1)}, bf16[64,3584]{1,0:T(8,128)(2,1)S(1)}, u32[]{:S(2)}, u32[]{:S(2)}) collective-permute-start(bf16[64,3584]{1,0:T(8,128)(2,1)} %shard_map.77.v), channel_id=1, source_target_pairs={{0,16},{8,24},{16,0},{24,8},{1,17},{9,25},{17,1},{25,9},{2,18},{10... | collective-permute-start | bytes 1376264 | tf_op jit(solution)/shard_map/ppermute | solution.py:22
  997.6 1.0 copy-start.1
  1004.9 0.8 copy-start.2
Sparse Core Ops, SparseCore 0:
  9.6 37.1 all-gather.2

commit v2 on v1

v2 whole, which is shorter than its diff:
```python
import functools

import jax
import jax.numpy as jnp
from jax import lax
from jax.experimental import pallas as pl
from jax.experimental.pallas import tpu as pltpu
from jax.sharding import PartitionSpec as P

D = 2048
FF = 14336
STEP = 1
FIX_ONE = 1.0 - 0.9**STEP
FIX_TWO = 1.0 - 0.95**STEP
TILE = 32
BAND = 256
SHARES = (2, 4, 4, 4, 4, 4, 4, 3, 2, 1)


def partner(value, axis, bit):
    mask = 2**bit
    pairs = [(source, source ^ mask) for source in range(lax.axis_size(axis))]
    return lax.ppermute(value, axis, pairs)


def first_kernel(bit, tok, up, old, first_old, second_old, *refs):
    old2, first_out, first2 = refs[:3]
    chunks = refs[3 : 3 + len(SHARES)]
    (up_all, tok_all, turned, grad, first, second, square, squares) = refs[3 + len(SHARES) : -12]
    (old_send, old_recv, up_send, up_recv, hop_send, hop_recv, first_send, first_recv) = refs[-12:-4]
    fan_send, fan_recv, sum_send, sum_recv_local = refs[-4:]
    sum_recv, local = sum_recv_local.at[0], sum_recv_local.at[1]
    group, half, part = (lax.axis_index(name) for name in ("replica", "dp", "tensor"))
    parts = lax.axis_size("tensor")
    per = parts // 2
    count, feats = tok.shape
    rows, cols = old.shape
    partner_at = {"replica": group ^ 2**bit}
    other_at = {"dp": 1 - half}
    slot = lax.rem(part, per)
    owned = part // per == half

    def lines(which):
        return pl.ds(pl.multiple_of(which * count, count), count)

    def place(which, column):
        return tok_all.at[lines(which), pl.ds(pl.multiple_of(column * feats, feats), feats)]

    def remote(source, target, send, recv, where):
        return pltpu.make_async_remote_copy(
            src_ref=source,
            dst_ref=target,
            send_sem=send,
            recv_sem=recv,
            device_id=where,
            device_id_type=pl.DeviceIdType.MESH,
        )

    peers = [{"tensor": lax.rem(part + step, parts)} for step in range(1, parts)]
    across = [
        {"dp": 1 - half, "tensor": lax.rem(part + step, parts)} for step in range(parts)
    ]
    barrier = pltpu.get_barrier_semaphore()
    for where in [partner_at] + peers + across:
        pl.semaphore_signal(
            barrier, inc=1, device_id=where, device_id_type=pl.DeviceIdType.MESH
        )
    pl.semaphore_wait(barrier, 2 * parts)

    send_old = remote(old, old2, old_send, old_recv, partner_at)
    send_old.start()
    send_hop = remote(tok, place(half, slot), hop_send, hop_recv, other_at)
    came_hop = remote(tok, place(1 - half, slot), hop_send, hop_recv, other_at)

    def fan(step, kind):
        which = 1 - half if kind else half
        return remote(
            place(which, slot) if kind else tok,
            place(which, slot),
            fan_send.at[step, kind],
            fan_recv.at[slot, kind],
            peers[step],
        )

    keep_tok = pltpu.make_async_copy(tok, place(half, slot), local.at[0])

    @pl.when(jnp.logical_not(owned))
    def _():
        send_hop.start()

    @pl.when(owned)
    def _():
        for step in range(parts - 1):
            fan(step, 0).start()
        keep_tok.start()

    send_up = remote(up, up_all.at[lines(half)], up_send, up_recv, other_at)
    came_up = remote(up, up_all.at[lines(1 - half)], up_send, up_recv, other_at)
    send_up.start()
    keep_up = pltpu.make_async_copy(up, up_all.at[lines(half)], local.at[1])
    keep_up.start()
    load_first = pltpu.make_async_copy(first_old, first, local.at[2])
    load_first.start()
    load_second = pltpu.make_async_copy(second_old, second, local.at[3])
    load_second.start()

    @pl.when(jnp.logical_not(owned))
    def _():
        send_hop.wait_send()

    @pl.when(owned)
    def _():
        came_hop.wait_recv()
        for step in range(parts - 1):
            fan(step, 1).start()
        for step in range(parts - 1):
            fan(step, 0).wait_send()
            fan(step, 1).wait_send()
        keep_tok.wait()

    for index in range(per):

        @pl.when(part != half * per + index)
        def _(index=index):
            for kind, which in enumerate((half, 1 - half)):
                remote(
                    tok,
                    place(which, index),
                    fan_send.at[0, kind],
                    fan_recv.at[index, kind],
                    peers[0],
                ).wait_recv()

    turned[...] = tok_all[...].T
    square[...] = jnp.zeros_like(square)
    keep_up.wait()
    send_up.wait_send()
    came_up.wait_recv()
    bands = rows // BAND

    @pl.loop(0, bands * (cols // BAND))
    def _(index):
        high = pl.ds(pl.multiple_of(lax.rem(index, bands) * BAND, BAND), BAND)
        wide = pl.ds(pl.multiple_of(index // bands * BAND, BAND), BAND)
        product = jnp.dot(turned[high, :], up_all[:, wide], preferred_element_type=jnp.float32)
        grad[high, wide] = product
        square[...] += jnp.sum((product * product).reshape(BAND // 8, 8, BAND), axis=0)

    rank = half * parts + part
    sums = [
        remote(square, squares.at[rank], sum_send.at[index], sum_recv.at[rank], where)
        for index, where in enumerate(peers + across)
    ]
    for copy in sums:
        copy.start()
    squares[rank] = square[...]
    load_first.wait()
    load_second.wait()
    for copy in sums:
        copy.wait_send()
    for index in range(2 * parts):

        @pl.when(rank != index)
        def _(index=index):
            remote(
                square, squares.at[index], sum_send.at[0], sum_recv.at[index], peers[0]
            ).wait_recv()

    total = jnp.sum(squares[...], axis=0)
    total = jnp.sum(jnp.sum(total, axis=1, keepdims=True), axis=0, keepdims=True)
    clip = jnp.minimum(1.0, 1.0 / jnp.sqrt(total / (D * FF) + 1e-06))

    @pl.loop(0, rows // 16)
    def _(index):
        high = pl.ds(pl.multiple_of(index * 16, 16), 16)
        scaled = clip * grad[high, :]
        first[high, :] = (0.9 * first[high, :].astype(jnp.float32) + 0.1 * scaled).astype(
            jnp.bfloat16
        )

    send_first = remote(first, first2, first_send, first_recv, partner_at)
    send_first.start()
    keeps = [pltpu.make_async_copy(first, first_out, local.at[0])]
    keeps[0].start()

    @pl.loop(0, rows // 16)
    def _(index):
        high = pl.ds(pl.multiple_of(index * 16, 16), 16)
        scaled = clip * grad[high, :]
        second[high, :] = (
            0.95 * second[high, :].astype(jnp.float32) + 0.05 * scaled * scaled
        ).astype(jnp.bfloat16)

    start = 0
    for index, chunk in enumerate(chunks):
        size = chunk.shape[0]
        keep = pltpu.make_async_copy(second.at[pl.ds(start, size)], chunk, local.at[1 + index])
        keep.start()
        keeps.append(keep)
        start += size
    for keep in keeps:
        keep.wait()
    send_old.wait()
    send_first.wait()


def first_phase(tokens, upstream, weights, first_moment, second_moment, bit):
    count, feats = tokens.shape
    rows, cols = weights.shape
    parts = lax.axis_size("tensor")
    anywhere = pl.BlockSpec(memory_space=pl.ANY)
    dma = pltpu.SemaphoreType.DMA
    whole = jax.ShapeDtypeStruct((rows, cols), jnp.bfloat16)
    sizes = [rows * share // sum(SHARES) for share in SHARES]
    wide = max(2 * parts, 1 + len(SHARES), 4)
    outs = pl.pallas_call(
        functools.partial(first_kernel, bit),
        in_specs=[anywhere] * 5,
        out_specs=(anywhere,) * (3 + len(sizes)),
        out_shape=(whole,) * 3
        + tuple(jax.ShapeDtypeStruct((size, cols), jnp.bfloat16) for size in sizes),
        scratch_shapes=[
            pltpu.VMEM((2 * count, cols), jnp.bfloat16),
            pltpu.VMEM((2 * count, feats * (parts // 2)), jnp.bfloat16),
            pltpu.VMEM((feats * (parts // 2), 2 * count), jnp.bfloat16),
            pltpu.VMEM((rows, cols), jnp.float32),
            pltpu.VMEM((rows, cols), jnp.bfloat16),
            pltpu.VMEM((rows, cols), jnp.bfloat16),
            pltpu.VMEM((8, BAND), jnp.float32),
            pltpu.VMEM((2 * parts, 8, BAND), jnp.float32),
        ]
        + [dma(())] * 8
        + [dma((parts - 1, 2)), dma((parts // 2, 2)), dma((2 * parts - 1,)), dma((2, wide))],
        cost_estimate=pl.CostEstimate(
            flops=4 * count * rows * cols, bytes_accessed=20 * rows * cols, transcendentals=0
        ),
        compiler_params=pltpu.CompilerParams(
            collective_id=0, has_side_effects=True, vmem_limit_bytes=62 * 2**20
        ),
    )(tokens, upstream, weights, first_moment, second_moment)
    return outs[0], outs[1], outs[2], outs[3:]


def gate_kernel(value, *refs):
    refs[-1][...] = value[...]


def gate(value, after):
    rows, cols = value.shape
    block = pl.BlockSpec((TILE, cols), lambda i: (i, 0))
    return pl.pallas_call(
        gate_kernel,
        grid=(rows // TILE,),
        in_specs=[block] + [pl.BlockSpec(memory_space=pl.ANY)] * len(after),
        out_specs=block,
        out_shape=jax.ShapeDtypeStruct((rows, cols), jnp.bfloat16),
        cost_estimate=pl.CostEstimate(
            flops=0, bytes_accessed=4 * rows * cols, transcendentals=0
        ),
        compiler_params=pltpu.CompilerParams(vmem_limit_bytes=60 * 2**20),
    )(value, *after)


def new_weights(old, first, second):
    old = old.astype(jnp.float32)
    first = first.astype(jnp.float32)
    second = second.astype(jnp.float32)
    update = first / FIX_ONE / (jnp.sqrt(second / FIX_TWO) + 1e-08)
    fresh = old - 0.05 * (update + 0.1 * old)
    return fresh.astype(jnp.bfloat16)


def mean(one, two):
    return (0.5 * (one.astype(jnp.float32) + two.astype(jnp.float32))).astype(jnp.bfloat16)


def mix_kernel(w, w2, m, m2, v, v2, *refs):
    out_w, out_m, out_v, done = refs[-4:]
    first, first2 = m[...], m2[...]
    second, second2 = v[...], v2[...]
    out_m[...] = mean(first, first2)
    out_v[...] = mean(second, second2)
    out_w[...] = mean(
        new_weights(w[...], first, second), new_weights(w2[...], first2, second2)
    )
    done[...] = jnp.zeros_like(done)


def mix_chunk(w, w2, m, m2, v, v2, held, start):
    rows, cols = v.shape
    first = start // TILE
    far = pl.BlockSpec((TILE, cols), lambda i: (first + i, 0))
    near = pl.BlockSpec((TILE, cols), lambda i: (i, 0))
    *outs, done = pl.pallas_call(
        mix_kernel,
        grid=(rows // TILE,),
        in_specs=[far, far, far, far, near, near]
        + [pl.BlockSpec(memory_space=pl.ANY)] * len(held),
        out_specs=(far, far, far, pl.BlockSpec((8, 128), lambda i: (0, 0))),
        out_shape=(jax.ShapeDtypeStruct(w.shape, jnp.bfloat16),) * 3
        + (jax.ShapeDtypeStruct((8, 128), jnp.float32),),
        input_output_aliases={6 + i: i for i in range(len(held))},
        cost_estimate=pl.CostEstimate(
            flops=30 * rows * cols, bytes_accessed=18 * rows * cols, transcendentals=4 * rows * cols
        ),
        compiler_params=pltpu.CompilerParams(vmem_limit_bytes=60 * 2**20),
    )(w, w2, m, m2, v, v2, *held)
    return outs, done


def body(tokens, grad_out, weights, first_moment, second_moment):
    bit = lax.axis_size("replica").bit_length() - 2
    weights = weights[0]
    weights2, first, first2, chunks = first_phase(
        tokens[0], grad_out[0], weights, first_moment[0], second_moment[0], bit
    )
    arrived, mixed, outs, start = [], [], (), 0
    for index, second in enumerate(chunks):
        if index >= 2:
            after = [arrived[index - 2]]
            if index >= 3:
                after.append(mixed[index - 3])
            second = gate(second, after)
        second2 = partner(second, "replica", bit)
        arrived.append(second2)
        outs, done = mix_chunk(weights, weights2, first, first2, second, second2, outs, start)
        mixed.append(done)
        start += second.shape[0]
    return tuple(out[None] for out in outs)


def solution(mesh):
    placed = P("replica", "dp", "tensor")
    return jax.shard_map(
        body,
        mesh=mesh,
        in_specs=(placed,) * 5,
        out_specs=(placed,) * 3,
        check_vma=False,
    )
```

time: 1020 us -> 960 us (0.941)
  Pallas kernels: 70.5 us -> 714 us
  waiting for transfers between devices: 863 us -> 232 us
  matrix products: 27.2 us -> 0 us
  blocking collectives: 14.6 us -> 0 us
  between operations: 14.8 us -> 0.7 us
  other arithmetic: 10.7 us -> 0 us
    pallas_call x4 -> x9, Pallas kernels: 25.5 us -> 660 us  [the longest x1 637 us: first_phase(): pl.pallas_call(functools.partial(first_kernel, bit), in_specs=[anywhere]...]
    ppermute x8 -> x10, waiting for transfers between devices: 826 us -> 232 us  [partner(): return lax.ppermute(value, axis, pairs)]
    all_gather x1 -> x0, waiting for transfers between devices: 35.9 us -> none  [body(): whole = lax.all_gather(tokens[0], 'tensor', axis=1, tiled=True)]
    dot_general x2 -> x0, matrix products: 27.2 us -> none  [contract(): lax.dot_general(one, two, (((0,), (0,)), ((), ())), preferred_element_typ...]
    psum x1 -> x0, blocking collectives: 14.6 us -> none  [body(): total = lax.psum(jnp.sum(grad * grad), ('dp', 'tensor'))]
    convert_element_type x1 -> x0, other arithmetic: 10.7 us -> none  [body(): (0.9 * first_moment.astype(jnp.float32) + 0.1 * (clip * grad)).astype(jnp...]
    pallas_call x4 -> x10, Pallas kernels: 45 us -> 53.6 us  [mix_chunk(): pl.pallas_call(mix_kernel, grid=(rows // TILE,), in_specs=[far, far, far,...]
  transfers between devices with their start and end apart: 9 -> 10, of which waited for: 7 -> 10; matrix products, arithmetic and copies ran while one was open for 4% -> 0% of each run, Pallas kernels for 7% -> 8%
where the time goes in v2:
time: 960 us; the launch traced here: 959 us
  Pallas kernels  714 us (74%)
  waiting for transfers between devices  232 us (24%)
    pallas_call x1, Pallas kernels, first_phase(): pl.pallas_call(functools.partial(first_kernel, bit), in_specs=[anywhere]...  637 us
    ppermute x10, waiting for transfers between devices, partner(): return lax.ppermute(value, axis, pairs)  232 us
    pallas_call x10, Pallas kernels, mix_chunk(): pl.pallas_call(mix_kernel, grid=(rows // TILE,), in_specs=[far, far, far,...  53.6 us
    pallas_call x8, Pallas kernels, gate(): pl.pallas_call(gate_kernel, grid=(rows // TILE,), in_specs=[block] + [pl....  22.9 us
  transfers between devices with their start and end apart: 10, of which 10 were waited for; matrix products, arithmetic and copies ran while one was open for 0% of the time, Pallas kernels for 8%

profile of v2, /device:TPU:0, one launch (start us, length us, event | category | flops | bytes accessed | tf_op | source)
XLA Modules:
  0.0 958.8 jit_solution(13812943573701416538)
XLA Ops:
  0.6 637.5 %shard_map.76 = (bf16[1024,3584]{1,0:T(8,128)(2,1)}, bf16[1024,3584]{1,0:T(8,128)(2,1)}, bf16[1024,3584]{1,0:T(8,128)(2,1)}, bf16[64,3584]{1,0:T(8,128)(2,1)}, b...) custom-call(bf16[1024,512]{1,0:T(8,128)(2,1)} %bitcast.25, ...), custom_call_target="tpu_custom_call" | custom-call | flops 15032385536 | bytes 73400320 | tf_op jit(solution)/shard_map/pallas_call | solution.py:216
  638.1 0.1 collective-permute-start.1
  638.2 2.9 collective-permute-start
  641.1 38.8 %collective-permute-done.1.v2.refs_0_ = bf16[64,3584]{1,0:T(8,128)(2,1)S(1)} collective-permute-done((bf16[64,3584]{1,0:T(8,128)(2,1)}, bf16[64,3584]{1,0:T(8,128)(2,1)S(1)}, u32[]{:S(2)}, u32[]{:S(2)}) %collective-permute-start.1) | collective-permute-done | bytes 458784 | tf_op jit(solution)/shard_map/ppermute | solution.py:23
  680.0 0.8 copy-done.7
  680.8 3.3 shard_map.79.v
  684.1 0.0 collective-permute-start.3
  684.1 3.8 shard_map.77
  687.9 31.4 %collective-permute-done.refs_0_.v2 = bf16[128,3584]{1,0:T(8,128)(2,1)S(1)} collective-permute-done((bf16[128,3584]{1,0:T(8,128)(2,1)}, bf16[128,3584]{1,0:T(8,128)(2,1)S(1)}, u32[]{:S(2)}, u32[]{:S(2)}) %collective-permute-start) | collective-permute-done | bytes 917536 | tf_op jit(solution)/shard_map/ppermute | solution.py:23
  719.3 1.0 copy-done.5
  720.3 3.3 shard_map.78.v
  723.6 0.0 collective-permute-start.2
  723.6 6.3 shard_map.80
  729.9 28.7 %collective-permute-done.3.v2.refs_0_ = bf16[128,3584]{1,0:T(8,128)(2,1)S(1)} collective-permute-done((bf16[128,3584]{1,0:T(8,128)(2,1)}, bf16[128,3584]{1,0:T(8,128)(2,1)S(1)}, u32[]{:S(2)}, u32[]{:S(2)}) %collective-permute-start.3) | collective-permute-done | bytes 917536 | tf_op jit(solution)/shard_map/ppermute | solution.py:23
  758.6 0.9 copy-done.4
  759.5 3.4 shard_map.83.v
  762.9 0.0 collective-permute-start.5
  762.9 6.3 shard_map.81
  769.2 28.8 %collective-permute-done.2.refs_0_.v2 = bf16[128,3584]{1,0:T(8,128)(2,1)S(1)} collective-permute-done((bf16[128,3584]{1,0:T(8,128)(2,1)}, bf16[128,3584]{1,0:T(8,128)(2,1)S(1)}, u32[]{:S(2)}, u32[]{:S(2)}) %collective-permute-start.2) | collective-permute-done | bytes 917536 | tf_op jit(solution)/shard_map/ppermute | solution.py:23
  797.9 0.9 copy-done.2
  798.9 3.3 shard_map.82.v
  802.2 0.0 collective-permute-start.4
  802.2 6.3 shard_map.84
  808.5 28.8 %collective-permute-done.5.v2.refs_0_ = bf16[128,3584]{1,0:T(8,128)(2,1)S(1)} collective-permute-done((bf16[128,3584]{1,0:T(8,128)(2,1)}, bf16[128,3584]{1,0:T(8,128)(2,1)S(1)}, u32[]{:S(2)}, u32[]{:S(2)}) %collective-permute-start.5) | collective-permute-done | bytes 917536 | tf_op jit(solution)/shard_map/ppermute | solution.py:23
  837.3 0.9 copy-done.3
  838.2 3.3 shard_map.87.v
  841.5 0.0 collective-permute-start.7
  841.5 6.3 shard_map.85
  847.8 28.8 %collective-permute-done.4.refs_0_.v2 = bf16[128,3584]{1,0:T(8,128)(2,1)S(1)} collective-permute-done((bf16[128,3584]{1,0:T(8,128)(2,1)}, bf16[128,3584]{1,0:T(8,128)(2,1)S(1)}, u32[]{:S(2)}, u32[]{:S(2)}) %collective-permute-start.4) | collective-permute-done | bytes 917536 | tf_op jit(solution)/shard_map/ppermute | solution.py:23
  876.6 0.9 copy-done
  877.5 2.8 shard_map.86.v
  880.3 0.0 collective-permute-start.6
  880.3 6.3 shard_map.88
  886.6 24.4 %collective-permute-done.7.v2.refs_0_ = bf16[128,3584]{1,0:T(8,128)(2,1)S(1)} collective-permute-done((bf16[128,3584]{1,0:T(8,128)(2,1)}, bf16[128,3584]{1,0:T(8,128)(2,1)S(1)}, u32[]{:S(2)}, u32[]{:S(2)}) %collective-permute-start.7) | collective-permute-done | bytes 917536 | tf_op jit(solution)/shard_map/ppermute | solution.py:23
  911.0 0.9 copy-done.1
  911.9 1.8 shard_map.91.v
  913.7 0.0 collective-permute-start.9
  913.7 6.3 shard_map.89
  920.0 15.6 %collective-permute-done.6.refs_0_.v2 = bf16[96,3584]{1,0:T(8,128)(2,1)S(1)} collective-permute-done((bf16[96,3584]{1,0:T(8,128)(2,1)}, bf16[96,3584]{1,0:T(8,128)(2,1)S(1)}, u32[]{:S(2)}, u32[]{:S(2)}) %collective-permute-start.6) | collective-permute-done | bytes 688160 | tf_op jit(solution)/shard_map/ppermute | solution.py:23
  935.6 0.9 copy-done.6
  936.4 1.6 shard_map.90.v
  938.1 5.4 shard_map.92
  943.5 6.8 collective-permute-done.9.v2
  950.3 0.8 copy-done.8
  951.1 3.8 shard_map.93
  954.9 0.3 collective-permute-done.8.v2
  955.1 0.7 copy-done.9
  955.9 2.9 shard_map.94
  (11 shorter events, 0.0 us)
Async XLA Ops:
  638.1 41.8 %collective-permute-start.1 = (bf16[64,3584]{1,0:T(8,128)(2,1)}, bf16[64,3584]{1,0:T(8,128)(2,1)S(1)}, u32[]{:S(2)}, u32[]{:S(2)}) collective-permute-start(bf16[64,3584]{1,0:T(8,128)(2,1)} %get-tuple-element.61.v), channel_id=1, source_target_pairs={{0,16},{8,24},{16,0},{24,8},{1,17},{9,25},{17,1},{25,9},{2,18},{10... | collective-permute-start | bytes 1376264 | tf_op jit(solution)/shard_map/ppermute | solution.py:23
  638.2 81.1 %collective-permute-start = (bf16[128,3584]{1,0:T(8,128)(2,1)}, bf16[128,3584]{1,0:T(8,128)(2,1)S(1)}, u32[]{:S(2)}, u32[]{:S(2)}) collective-permute-start(bf16[128,3584]{1,0:T(8,128)(2,1)} %get-tuple-element.60.v), channel_id=1, source_target_pairs={{0,16},{8,24},{16,0},{24,8},{1,17},{9,25},{17,1},{25,9},{2,18},{10... | collective-permute-start | bytes 2752520 | tf_op jit(solution)/shard_map/ppermute | solution.py:23
  680.0 0.8 copy-start.7
  684.1 74.5 %collective-permute-start.3 = (bf16[128,3584]{1,0:T(8,128)(2,1)}, bf16[128,3584]{1,0:T(8,128)(2,1)S(1)}, u32[]{:S(2)}, u32[]{:S(2)}) collective-permute-start(bf16[128,3584]{1,0:T(8,128)(2,1)} %shard_map.79.v), channel_id=1, source_target_pairs={{0,16},{8,24},{16,0},{24,8},{1,17},{9,25},{17,1},{25,9},{2,18},{10... | collective-permute-start | bytes 2752520 | tf_op jit(solution)/shard_map/ppermute | solution.py:23
  719.3 1.0 copy-start.5
  723.6 74.4 %collective-permute-start.2 = (bf16[128,3584]{1,0:T(8,128)(2,1)}, bf16[128,3584]{1,0:T(8,128)(2,1)S(1)}, u32[]{:S(2)}, u32[]{:S(2)}) collective-permute-start(bf16[128,3584]{1,0:T(8,128)(2,1)} %shard_map.78.v), channel_id=1, source_target_pairs={{0,16},{8,24},{16,0},{24,8},{1,17},{9,25},{17,1},{25,9},{2,18},{10... | collective-permute-start | bytes 2752520 | tf_op jit(solution)/shard_map/ppermute | solution.py:23
  758.6 0.9 copy-start.4
  762.9 74.4 %collective-permute-start.5 = (bf16[128,3584]{1,0:T(8,128)(2,1)}, bf16[128,3584]{1,0:T(8,128)(2,1)S(1)}, u32[]{:S(2)}, u32[]{:S(2)}) collective-permute-start(bf16[128,3584]{1,0:T(8,128)(2,1)} %shard_map.83.v), channel_id=1, source_target_pairs={{0,16},{8,24},{16,0},{24,8},{1,17},{9,25},{17,1},{25,9},{2,18},{10... | collective-permute-start | bytes 2752520 | tf_op jit(solution)/shard_map/ppermute | solution.py:23
  797.9 0.9 copy-start.2
  802.2 74.4 %collective-permute-start.4 = (bf16[128,3584]{1,0:T(8,128)(2,1)}, bf16[128,3584]{1,0:T(8,128)(2,1)S(1)}, u32[]{:S(2)}, u32[]{:S(2)}) collective-permute-start(bf16[128,3584]{1,0:T(8,128)(2,1)} %shard_map.82.v), channel_id=1, source_target_pairs={{0,16},{8,24},{16,0},{24,8},{1,17},{9,25},{17,1},{25,9},{2,18},{10... | collective-permute-start | bytes 2752520 | tf_op jit(solution)/shard_map/ppermute | solution.py:23
  837.3 0.9 copy-start.3
  841.5 69.5 %collective-permute-start.7 = (bf16[128,3584]{1,0:T(8,128)(2,1)}, bf16[128,3584]{1,0:T(8,128)(2,1)S(1)}, u32[]{:S(2)}, u32[]{:S(2)}) collective-permute-start(bf16[128,3584]{1,0:T(8,128)(2,1)} %shard_map.87.v), channel_id=1, source_target_pairs={{0,16},{8,24},{16,0},{24,8},{1,17},{9,25},{17,1},{25,9},{2,18},{10... | collective-permute-start | bytes 2752520 | tf_op jit(solution)/shard_map/ppermute | solution.py:23
  876.6 0.9 copy-start
  880.3 55.3 %collective-permute-start.6 = (bf16[96,3584]{1,0:T(8,128)(2,1)}, bf16[96,3584]{1,0:T(8,128)(2,1)S(1)}, u32[]{:S(2)}, u32[]{:S(2)}) collective-permute-start(bf16[96,3584]{1,0:T(8,128)(2,1)} %shard_map.86.v), channel_id=1, source_target_pairs={{0,16},{8,24},{16,0},{24,8},{1,17},{9,25},{17,1},{25,9},{2,18},{10... | collective-permute-start | bytes 2064392 | tf_op jit(solution)/shard_map/ppermute | solution.py:23
  911.0 0.9 copy-start.1
  913.7 36.6 %collective-permute-start.9 = (bf16[64,3584]{1,0:T(8,128)(2,1)}, bf16[64,3584]{1,0:T(8,128)(2,1)S(1)}, u32[]{:S(2)}, u32[]{:S(2)}) collective-permute-start(bf16[64,3584]{1,0:T(8,128)(2,1)} %shard_map.91.v), channel_id=1, source_target_pairs={{0,16},{8,24},{16,0},{24,8},{1,17},{9,25},{17,1},{25,9},{2,18},{10... | collective-permute-start | bytes 1376264 | tf_op jit(solution)/shard_map/ppermute | solution.py:23
  935.6 0.9 copy-start.6
  938.1 17.1 %collective-permute-start.8 = (bf16[32,3584]{1,0:T(8,128)(2,1)}, bf16[32,3584]{1,0:T(8,128)(2,1)S(1)}, u32[]{:S(2)}, u32[]{:S(2)}) collective-permute-start(bf16[32,3584]{1,0:T(8,128)(2,1)} %shard_map.90.v), channel_id=1, source_target_pairs={{0,16},{8,24},{16,0},{24,8},{1,17},{9,25},{17,1},{25,9},{2,18},{10... | collective-permute-start | bytes 688136 | tf_op jit(solution)/shard_map/ppermute | solution.py:23
  950.3 0.8 copy-start.8
  955.1 0.7 copy-start.9

commit v3 on v2

--- a/solution.py
+++ b/solution.py
@@ -1,5 +1,3 @@
-import functools
-
 import jax
 import jax.numpy as jnp
 from jax import lax
@@ -14,7 +12,7 @@
 FIX_TWO = 1.0 - 0.95**STEP
 TILE = 32
 BAND = 256
-SHARES = (2, 4, 4, 4, 4, 4, 4, 3, 2, 1)
+SHARES = (20, 4, 3, 3, 2)
 
 
 def partner(value, axis, bit):
@@ -23,19 +21,17 @@
     return lax.ppermute(value, axis, pairs)
 
 
-def first_kernel(bit, tok, up, old, first_old, second_old, *refs):
-    old2, first_out, first2 = refs[:3]
-    chunks = refs[3 : 3 + len(SHARES)]
-    (up_all, tok_all, turned, grad, first, second, square, squares) = refs[3 + len(SHARES) : -12]
-    (old_send, old_recv, up_send, up_recv, hop_send, hop_recv, first_send, first_recv) = refs[-12:-4]
+def first_kernel(tok, up, first_old, second_old, *refs):
+    first_out, *chunks = refs[: 1 + len(SHARES)]
+    (up_all, tok_all, turned, grad, first, second, square, squares) = refs[1 + len(SHARES) : -8]
+    up_send, up_recv, hop_send, hop_recv = refs[-8:-4]
     fan_send, fan_recv, sum_send, sum_recv_local = refs[-4:]
     sum_recv, local = sum_recv_local.at[0], sum_recv_local.at[1]
-    group, half, part = (lax.axis_index(name) for name in ("replica", "dp", "tensor"))
+    half, part = lax.axis_index("dp"), lax.axis_index("tensor")
     parts = lax.axis_size("tensor")
     per = parts // 2
     count, feats = tok.shape
-    rows, cols = old.shape
-    partner_at = {"replica": group ^ 2**bit}
+    rows, cols = first_old.shape
     other_at = {"dp": 1 - half}
     slot = lax.rem(part, per)
     owned = part // per == half
@@ -61,14 +57,12 @@
         {"dp": 1 - half, "tensor": lax.rem(part + step, parts)} for step in range(parts)
     ]
     barrier = pltpu.get_barrier_semaphore()
-    for where in [partner_at] + peers + across:
+    for where in peers + across:
         pl.semaphore_signal(
             barrier, inc=1, device_id=where, device_id_type=pl.DeviceIdType.MESH
         )
-    pl.semaphore_wait(barrier, 2 * parts)
-
-    send_old = remote(old, old2, old_send, old_recv, partner_at)
-    send_old.start()
+    pl.semaphore_wait(barrier, 2 * parts - 1)
+
     send_hop = remote(tok, place(half, slot), hop_send, hop_recv, other_at)
     came_hop = remote(tok, place(1 - half, slot), hop_send, hop_recv, other_at)
 
@@ -178,8 +172,6 @@
             jnp.bfloat16
         )
 
-    send_first = remote(first, first2, first_send, first_recv, partner_at)
-    send_first.start()
     keeps = [pltpu.make_async_copy(first, first_out, local.at[0])]
     keeps[0].start()
 
@@ -200,13 +192,11 @@
         start += size
     for keep in keeps:
         keep.wait()
-    send_old.wait()
-    send_first.wait()
-
-
-def first_phase(tokens, upstream, weights, first_moment, second_moment, bit):
+
+
+def first_phase(tokens, upstream, first_moment, second_moment):
     count, feats = tokens.shape
-    rows, cols = weights.shape
+    rows, cols = first_moment.shape
     parts = lax.axis_size("tensor")
     anywhere = pl.BlockSpec(memory_space=pl.ANY)
     dma = pltpu.SemaphoreType.DMA
@@ -214,10 +204,10 @@
     sizes = [rows * share // sum(SHARES) for share in SHARES]
     wide = max(2 * parts, 1 + len(SHARES), 4)
     outs = pl.pallas_call(
-        functools.partial(first_kernel, bit),
-        in_specs=[anywhere] * 5,
-        out_specs=(anywhere,) * (3 + len(sizes)),
-        out_shape=(whole,) * 3
+        first_kernel,
+        in_specs=[anywhere] * 4,
+        out_specs=(anywhere,) * (1 + len(sizes)),
+        out_shape=(whole,)
         + tuple(jax.ShapeDtypeStruct((size, cols), jnp.bfloat16) for size in sizes),
         scratch_shapes=[
             pltpu.VMEM((2 * count, cols), jnp.bfloat16),
@@ -229,7 +219,7 @@
             pltpu.VMEM((8, BAND), jnp.float32),
             pltpu.VMEM((2 * parts, 8, BAND), jnp.float32),
         ]
-        + [dma(())] * 8
+        + [dma(())] * 4
         + [dma((parts - 1, 2)), dma((parts // 2, 2)), dma((2 * parts - 1,)), dma((2, wide))],
         cost_estimate=pl.CostEstimate(
             flops=4 * count * rows * cols, bytes_accessed=20 * rows * cols, transcendentals=0
@@ -237,8 +227,8 @@
         compiler_params=pltpu.CompilerParams(
             collective_id=0, has_side_effects=True, vmem_limit_bytes=62 * 2**20
         ),
-    )(tokens, upstream, weights, first_moment, second_moment)
-    return outs[0], outs[1], outs[2], outs[3:]
+    )(tokens, upstream, first_moment, second_moment)
+    return outs[0], outs[1:]
 
 
 def gate_kernel(value, *refs):
@@ -311,16 +301,17 @@
 def body(tokens, grad_out, weights, first_moment, second_moment):
     bit = lax.axis_size("replica").bit_length() - 2
     weights = weights[0]
-    weights2, first, first2, chunks = first_phase(
-        tokens[0], grad_out[0], weights, first_moment[0], second_moment[0], bit
-    )
+    weights2 = partner(weights, "replica", bit)
+    first, chunks = first_phase(tokens[0], grad_out[0], first_moment[0], second_moment[0])
+    first2 = partner(first, "replica", bit)
     arrived, mixed, outs, start = [], [], (), 0
+    waits = (weights2, 0, first2, 1, 2)
     for index, second in enumerate(chunks):
-        if index >= 2:
-            after = [arrived[index - 2]]
-            if index >= 3:
-                after.append(mixed[index - 3])
-            second = gate(second, after)
+        wait = waits[index]
+        after = [arrived[wait] if isinstance(wait, int) else wait]
+        if index >= 3:
+            after.append(mixed[index - 3])
+        second = gate(second, after)
         second2 = partner(second, "replica", bit)
         arrived.append(second2)
         outs, done = mix_chunk(weights, weights2, first, first2, second, second2, outs, start)

time: 960 us -> 962 us (level)
  waiting for transfers between devices: 232 us -> 656 us
  Pallas kernels: 714 us -> 293 us
    ppermute x10 -> x7, waiting for transfers between devices: 232 us -> 656 us  [partner(): return lax.ppermute(value, axis, pairs)]
    pallas_call x1, Pallas kernels: 637 us -> 223 us  [first_phase(): pl.pallas_call(first_kernel, in_specs=[anywhere] * 4, out_specs=(anywhere...]
    pallas_call x10 -> x5, Pallas kernels: 53.6 us -> 47.1 us  [mix_chunk(): pl.pallas_call(mix_kernel, grid=(rows // TILE,), in_specs=[far, far, far,...]
    pallas_call x8 -> x5, Pallas kernels: 22.9 us -> 22.9 us  [gate(): pl.pallas_call(gate_kernel, grid=(rows // TILE,), in_specs=[block] + [pl....]
  transfers between devices with their start and end apart: 10 -> 7, of which waited for: 10 -> 6; matrix products, arithmetic and copies ran while one was open for 0% -> 0% of each run, Pallas kernels for 8% -> 30%
where the time goes in v3:
time: 962 us; the launch traced here: 960 us
  waiting for transfers between devices  656 us (68%)
  Pallas kernels  293 us (30%)
    ppermute x7, waiting for transfers between devices, partner(): return lax.ppermute(value, axis, pairs)  656 us
    pallas_call x1, Pallas kernels, first_phase(): pl.pallas_call(first_kernel, in_specs=[anywhere] * 4, out_specs=(anywhere...  223 us
    pallas_call x5, Pallas kernels, mix_chunk(): pl.pallas_call(mix_kernel, grid=(rows // TILE,), in_specs=[far, far, far,...  47.1 us
    pallas_call x5, Pallas kernels, gate(): pl.pallas_call(gate_kernel, grid=(rows // TILE,), in_specs=[block] + [pl....  22.9 us
  transfers between devices with their start and end apart: 7, of which 6 were waited for; matrix products, arithmetic and copies ran while one was open for 0% of the time, Pallas kernels for 30%

profile of v3, /device:TPU:0, one launch (start us, length us, event | category | flops | bytes accessed | tf_op | source)
XLA Modules:
  0.0 960.4 jit_solution(9119933790125064591)
XLA Ops:
  0.6 4.1 collective-permute-start
  4.7 222.6 %shard_map.76 = (bf16[1024,3584]{1,0:T(8,128)(2,1)}, bf16[640,3584]{1,0:T(8,128)(2,1)}, bf16[128,3584]{1,0:T(8,128)(2,1)}, bf16[96,3584]{1,0:T(8,128)(2,1)}, bf1...) custom-call(bf16[1024,512]{1,0:T(8,128)(2,1)} %bitcast.20, bf16[1024,3584]{1,0:T(8,128)(2,1)} %bitcast.17, ...), custom_call_target="tpu_custom_call" | custom-call | flops 15032385536 | bytes 73400320 | tf_op jit(solution)/shard_map/pallas_call | solution.py:206
  227.4 0.4 collective-permute-start.1
  227.8 250.7 %collective-permute-done.refs_0_.w2 = bf16[1024,3584]{1,0:T(8,128)(2,1)} collective-permute-done((bf16[1024,3584]{1,0:T(8,128)(2,1)}, bf16[1024,3584]{1,0:T(8,128)(2,1)}, u32[]{:S(2)}, u32[]{:S(2)}) %collective-permute-start) | collective-permute-done | bytes 7340064 | tf_op jit(solution)/shard_map/ppermute | solution.py:21
  478.5 12.2 %shard_map.78.v = bf16[640,3584]{1,0:T(8,128)(2,1)} custom-call(bf16[640,3584]{1,0:T(8,128)(2,1)} %get-tuple-element.30.value, bf16[1024,3584]{1,0:T(8,128)(2,1)} %collective-permute-done.refs_0_.w2), custom_call_target="tpu_custom_call" | custom-call | bytes 9175040 | tf_op jit(solution)/shard_map/pallas_call | solution.py:241
  490.7 0.0 collective-permute-start.3
  490.7 340.8 %collective-permute-done.3.refs_0_.v2 = bf16[640,3584]{1,0:T(8,128)(2,1)} collective-permute-done((bf16[640,3584]{1,0:T(8,128)(2,1)}, bf16[640,3584]{1,0:T(8,128)(2,1)}, u32[]{:S(2)}, u32[]{:S(2)}) %collective-permute-start.3) | collective-permute-done | bytes 4587552 | tf_op jit(solution)/shard_map/ppermute | solution.py:21
  831.5 3.3 shard_map.79.v
  834.9 0.0 collective-permute-start.4
  834.9 0.0 collective-permute-done.1.refs_0_.m2
  834.9 2.8 shard_map.77.v
  837.7 2.9 collective-permute-start.2
  840.6 26.2 %shard_map.80 = (bf16[1024,3584]{1,0:T(8,128)(2,1)}, bf16[1024,3584]{1,0:T(8,128)(2,1)}, bf16[1024,3584]{1,0:T(8,128)(2,1)}, f32[8,128]{1,0:T(8,128)}) custom-call(bf16[1024,3584]{1,0:T(8,128)(2,1)} %bitcast.9, bf16[1024,3584]{1,0:T(8,128)(2,1)} %collective-permute-done.refs_0_.w2, bf16[1024,3584]{1,0:T(8,128)(2,1)} %get-tuple-element.26.m, ...), custom_call_target="tpu_custom_call" | custom-call | flops 68812800 | bytes 41287680 | tf_op jit(solution)/shard_map/pallas_call | solution.py:284
  866.7 26.9 %collective-permute-done.4.v2.refs_0_ = bf16[128,3584]{1,0:T(8,128)(2,1)S(1)} collective-permute-done((bf16[128,3584]{1,0:T(8,128)(2,1)}, bf16[128,3584]{1,0:T(8,128)(2,1)S(1)}, u32[]{:S(2)}, u32[]{:S(2)}) %collective-permute-start.4) | collective-permute-done | bytes 917536 | tf_op jit(solution)/shard_map/ppermute | solution.py:21
  893.7 0.0 copy-start
  893.7 0.9 copy-done
  894.6 2.8 shard_map.83.v
  897.4 0.0 collective-permute-start.6
  897.4 6.3 shard_map.81
  903.7 19.4 %collective-permute-done.2.refs_0_.v2 = bf16[96,3584]{1,0:T(8,128)(2,1)S(1)} collective-permute-done((bf16[96,3584]{1,0:T(8,128)(2,1)}, bf16[96,3584]{1,0:T(8,128)(2,1)S(1)}, u32[]{:S(2)}, u32[]{:S(2)}) %collective-permute-start.2) | collective-permute-done | bytes 688160 | tf_op jit(solution)/shard_map/ppermute | solution.py:21
  923.2 0.0 copy-start.1
  923.2 0.9 copy-done.1
  924.0 1.8 shard_map.82.v
  925.8 0.0 collective-permute-start.5
  925.8 5.4 shard_map.84
  931.2 16.5 %collective-permute-done.6.v2 = bf16[96,3584]{1,0:T(8,128)(2,1)S(1)} collective-permute-done((bf16[96,3584]{1,0:T(8,128)(2,1)}, bf16[96,3584]{1,0:T(8,128)(2,1)S(1)}, u32[]{:S(2)}, u32[]{:S(2)}) %collective-permute-start.6) | collective-permute-done | bytes 688160 | tf_op jit(solution)/shard_map/ppermute | solution.py:21
  947.7 0.0 copy-start.2
  947.7 0.9 copy-done.2
  948.6 5.4 shard_map.85
  954.0 1.8 collective-permute-done.5.v2
  955.8 0.0 copy-start.3
  955.8 0.8 copy-done.3
  956.6 3.8 shard_map.86
Async XLA Ops:
  0.6 477.8 %collective-permute-start = (bf16[1024,3584]{1,0:T(8,128)(2,1)}, bf16[1024,3584]{1,0:T(8,128)(2,1)}, u32[]{:S(2)}, u32[]{:S(2)}) collective-permute-start(bf16[1024,3584]{1,0:T(8,128)(2,1)} %bitcast.8), channel_id=1, source_target_pairs={{0,16},{8,24},{16,0},{24,8},{1,17},{9,25},{17,1},{25,9},{2,18},{10... | collective-permute-start | bytes 22020104 | tf_op jit(solution)/shard_map/ppermute | solution.py:21
  227.4 607.5 %collective-permute-start.1 = (bf16[1024,3584]{1,0:T(8,128)(2,1)}, bf16[1024,3584]{1,0:T(8,128)(2,1)}, u32[]{:S(2)}, u32[]{:S(2)}) collective-permute-start(bf16[1024,3584]{1,0:T(8,128)(2,1)} %get-tuple-element.26.m), channel_id=1, source_target_pairs={{0,16},{8,24},{16,0},{24,8},{1,17},{9,25},{17,1},{25,9},{2,18},{10... | collective-permute-start | bytes 22020104 | tf_op jit(solution)/shard_map/ppermute | solution.py:21
  490.7 340.8 %collective-permute-start.3 = (bf16[640,3584]{1,0:T(8,128)(2,1)}, bf16[640,3584]{1,0:T(8,128)(2,1)}, u32[]{:S(2)}, u32[]{:S(2)}) collective-permute-start(bf16[640,3584]{1,0:T(8,128)(2,1)} %shard_map.78.v), channel_id=1, source_target_pairs={{0,16},{8,24},{16,0},{24,8},{1,17},{9,25},{17,1},{25,9},{2,18},{10... | collective-permute-start | bytes 13762568 | tf_op jit(solution)/shard_map/ppermute | solution.py:21
  834.9 58.8 %collective-permute-start.4 = (bf16[128,3584]{1,0:T(8,128)(2,1)}, bf16[128,3584]{1,0:T(8,128)(2,1)S(1)}, u32[]{:S(2)}, u32[]{:S(2)}) collective-permute-start(bf16[128,3584]{1,0:T(8,128)(2,1)} %shard_map.79.v), channel_id=1, source_target_pairs={{0,16},{8,24},{16,0},{24,8},{1,17},{9,25},{17,1},{25,9},{2,18},{10... | collective-permute-start | bytes 2752520 | tf_op jit(solution)/shard_map/ppermute | solution.py:21
  837.7 85.5 %collective-permute-start.2 = (bf16[96,3584]{1,0:T(8,128)(2,1)}, bf16[96,3584]{1,0:T(8,128)(2,1)S(1)}, u32[]{:S(2)}, u32[]{:S(2)}) collective-permute-start(bf16[96,3584]{1,0:T(8,128)(2,1)} %shard_map.77.v), channel_id=1, source_target_pairs={{0,16},{8,24},{16,0},{24,8},{1,17},{9,25},{17,1},{25,9},{2,18},{10... | collective-permute-start | bytes 2064392 | tf_op jit(solution)/shard_map/ppermute | solution.py:21
  893.7 0.9 copy-start
  897.4 50.3 %collective-permute-start.6 = (bf16[96,3584]{1,0:T(8,128)(2,1)}, bf16[96,3584]{1,0:T(8,128)(2,1)S(1)}, u32[]{:S(2)}, u32[]{:S(2)}) collective-permute-start(bf16[96,3584]{1,0:T(8,128)(2,1)} %shard_map.83.v), channel_id=1, source_target_pairs={{0,16},{8,24},{16,0},{24,8},{1,17},{9,25},{17,1},{25,9},{2,18},{10... | collective-permute-start | bytes 2064392 | tf_op jit(solution)/shard_map/ppermute | solution.py:21
  923.2 0.9 copy-start.1
  925.8 30.0 %collective-permute-start.5 = (bf16[64,3584]{1,0:T(8,128)(2,1)}, bf16[64,3584]{1,0:T(8,128)(2,1)S(1)}, u32[]{:S(2)}, u32[]{:S(2)}) collective-permute-start(bf16[64,3584]{1,0:T(8,128)(2,1)} %shard_map.82.v), channel_id=1, source_target_pairs={{0,16},{8,24},{16,0},{24,8},{1,17},{9,25},{17,1},{25,9},{2,18},{10... | collective-permute-start | bytes 1376264 | tf_op jit(solution)/shard_map/ppermute | solution.py:21
  947.7 0.9 copy-start.2
  955.8 0.8 copy-start.3

commit v4 on v3

--- a/solution.py
+++ b/solution.py
@@ -18,6 +18,13 @@
 def partner(value, axis, bit):
     mask = 2**bit
     pairs = [(source, source ^ mask) for source in range(lax.axis_size(axis))]
+    return lax.ppermute(value, axis, pairs)
+
+
+def back(value, axis):
+    size = lax.axis_size(axis)
+    step = size // 4
+    pairs = [(source, (source - step) % size) for source in range(size)]
     return lax.ppermute(value, axis, pairs)
 
 
@@ -311,8 +318,11 @@
         after = [arrived[wait] if isinstance(wait, int) else wait]
         if index >= 3:
             after.append(mixed[index - 3])
-        second = gate(second, after)
-        second2 = partner(second, "replica", bit)
+        if index:
+            second = gate(second, after)
+            second2 = partner(second, "replica", bit)
+        else:
+            second2 = back(back(second, "replica"), "replica")
         arrived.append(second2)
         outs, done = mix_chunk(weights, weights2, first, first2, second, second2, outs, start)
         mixed.append(done)

time: 962 us -> 1180 us (1.23)
  starting transfers between devices: 7.43 us -> 325 us
  waiting for transfers between devices: 656 us -> 569 us
    ppermute x7 -> x6, waiting for transfers between devices: 656 us -> 64.9 us  [partner(): return lax.ppermute(value, axis, pairs)]
    ppermute x0 -> x2, waiting for transfers between devices: none -> 505 us  [back(): return lax.ppermute(value, axis, pairs)]
    ppermute x7 -> x6, starting transfers between devices: 7.43 us -> 317 us  [partner(): return lax.ppermute(value, axis, pairs)]
    pallas_call x5 -> x4, Pallas kernels: 22.9 us -> 10.7 us  [gate(): pl.pallas_call(gate_kernel, grid=(rows // TILE,), in_specs=[block] + [pl....]
  transfers between devices with their start and end apart: 7 -> 8, of which waited for: 6 -> 6; matrix products, arithmetic and copies ran while one was open for 0% -> 0% of each run, Pallas kernels for 30% -> 5%
where the time goes in v4:
time: 1180 us
  waiting for transfers between devices  569 us (48%)
  starting transfers between devices  325 us (28%)
  Pallas kernels  282 us (24%)
    ppermute x2, waiting for transfers between devices, back(): return lax.ppermute(value, axis, pairs)  505 us
    ppermute x6, starting transfers between devices, partner(): return lax.ppermute(value, axis, pairs)  317 us
    pallas_call x1, Pallas kernels, first_phase(): pl.pallas_call(first_kernel, in_specs=[anywhere] * 4, out_specs=(anywhere...  224 us
    ppermute x6, waiting for transfers between devices, partner(): return lax.ppermute(value, axis, pairs)  64.9 us
    pallas_call x5, Pallas kernels, mix_chunk(): pl.pallas_call(mix_kernel, grid=(rows // TILE,), in_specs=[far, far, far,...  47.1 us
  transfers between devices with their start and end apart: 8, of which 6 were waited for; matrix products, arithmetic and copies ran while one was open for 0% of the time, Pallas kernels for 5%

profile of v4, /device:TPU:0, one launch (start us, length us, event | category | flops | bytes accessed | tf_op | source)
XLA Modules:
  0.0 1180.4 jit_solution(10145543098103056437)
XLA Ops:
  0.6 224.2 %shard_map.76 = (bf16[1024,3584]{1,0:T(8,128)(2,1)}, bf16[640,3584]{1,0:T(8,128)(2,1)}, bf16[128,3584]{1,0:T(8,128)(2,1)}, bf16[96,3584]{1,0:T(8,128)(2,1)}, bf1...) custom-call(bf16[1024,512]{1,0:T(8,128)(2,1)} %bitcast.20, bf16[1024,3584]{1,0:T(8,128)(2,1)} %bitcast.17, ...), custom_call_target="tpu_custom_call" | custom-call | flops 15032385536 | bytes 73400320 | tf_op jit(solution)/shard_map/pallas_call | solution.py:213
  224.8 3.7 collective-permute-start.3
  228.5 0.0 collective-permute-start.1
  228.5 2.9 collective-permute-start
  231.4 96.8 %collective-permute-done.3 = bf16[640,3584]{1,0:T(8,128)(2,1)S(1)} collective-permute-done((bf16[640,3584]{1,0:T(8,128)(2,1)}, bf16[640,3584]{1,0:T(8,128)(2,1)S(1)}, u32[]{:S(2)}, u32[]{:S(2)}) %collective-permute-start.3) | collective-permute-done | bytes 4587552 | tf_op jit(solution)/shard_map/ppermute | solution.py:28
  328.2 4.2 collective-permute-start.4
  332.4 407.7 %collective-permute-done.4.refs_0_.v2 = bf16[640,3584]{1,0:T(8,128)(2,1)} collective-permute-done((bf16[640,3584]{1,0:T(8,128)(2,1)S(1)}, bf16[640,3584]{1,0:T(8,128)(2,1)}, u32[]{:S(2)}, u32[]{:S(2)}) %collective-permute-start.4) | collective-permute-done | bytes 4587552 | tf_op jit(solution)/shard_map/ppermute | solution.py:28
  740.1 3.3 shard_map.78.v
  743.5 314.0 %collective-permute-start.5 = (bf16[128,3584]{1,0:T(8,128)(2,1)}, bf16[128,3584]{1,0:T(8,128)(2,1)S(1)}, u32[]{:S(2)}, u32[]{:S(2)}) collective-permute-start(bf16[128,3584]{1,0:T(8,128)(2,1)} %shard_map.78.v), channel_id=1, source_target_pairs={{0,16},{8,24},{16,0},{24,8},{1,17},{9,25},{17,1},{25,9},{2,18},{10... | collective-permute-start | bytes 2752520 | tf_op jit(solution)/shard_map/ppermute | solution.py:21
  1057.4 0.0 collective-permute-done.1.refs_0_.m2
  1057.4 2.8 shard_map.77.v
  1060.2 0.0 collective-permute-start.2
  1060.2 0.0 collective-permute-done.w2
  1060.2 26.2 %shard_map.79 = (bf16[1024,3584]{1,0:T(8,128)(2,1)}, bf16[1024,3584]{1,0:T(8,128)(2,1)}, bf16[1024,3584]{1,0:T(8,128)(2,1)}, f32[8,128]{1,0:T(8,128)}) custom-call(bf16[1024,3584]{1,0:T(8,128)(2,1)} %bitcast.9, bf16[1024,3584]{1,0:T(8,128)(2,1)} %collective-permute-done.w2, bf16[1024,3584]{1,0:T(8,128)(2,1)} %get-tuple-element.26.m, ...), custom_call_target="tpu_custom_call" | custom-call | flops 68812800 | bytes 41287680 | tf_op jit(solution)/shard_map/pallas_call | solution.py:291
  1086.4 26.9 %collective-permute-done.5.v2.refs_0_ = bf16[128,3584]{1,0:T(8,128)(2,1)S(1)} collective-permute-done((bf16[128,3584]{1,0:T(8,128)(2,1)}, bf16[128,3584]{1,0:T(8,128)(2,1)S(1)}, u32[]{:S(2)}, u32[]{:S(2)}) %collective-permute-start.5) | collective-permute-done | bytes 917536 | tf_op jit(solution)/shard_map/ppermute | solution.py:21
  1113.3 0.0 copy-start
  1113.3 0.9 copy-done
  1114.3 2.8 shard_map.82.v
  1117.1 0.0 collective-permute-start.7
  1117.1 6.3 shard_map.80
  1123.3 19.5 %collective-permute-done.2.refs_0_.v2 = bf16[96,3584]{1,0:T(8,128)(2,1)S(1)} collective-permute-done((bf16[96,3584]{1,0:T(8,128)(2,1)}, bf16[96,3584]{1,0:T(8,128)(2,1)S(1)}, u32[]{:S(2)}, u32[]{:S(2)}) %collective-permute-start.2) | collective-permute-done | bytes 688160 | tf_op jit(solution)/shard_map/ppermute | solution.py:21
  1142.8 0.0 copy-start.1
  1142.8 0.9 copy-done.1
  1143.7 1.8 shard_map.81.v
  1145.4 0.0 collective-permute-start.6
  1145.5 5.4 shard_map.83
  1150.9 16.5 %collective-permute-done.7.v2 = bf16[96,3584]{1,0:T(8,128)(2,1)S(1)} collective-permute-done((bf16[96,3584]{1,0:T(8,128)(2,1)}, bf16[96,3584]{1,0:T(8,128)(2,1)S(1)}, u32[]{:S(2)}, u32[]{:S(2)}) %collective-permute-start.7) | collective-permute-done | bytes 688160 | tf_op jit(solution)/shard_map/ppermute | solution.py:21
  1167.4 0.0 copy-start.2
  1167.4 0.9 copy-done.2
  1168.3 5.4 shard_map.84
  1173.7 2.1 collective-permute-done.6.v2
  1175.8 0.0 copy-start.3
  1175.8 0.8 copy-done.3
  1176.6 3.8 shard_map.85
Async XLA Ops:
  224.8 103.4 %collective-permute-start.3 = (bf16[640,3584]{1,0:T(8,128)(2,1)}, bf16[640,3584]{1,0:T(8,128)(2,1)S(1)}, u32[]{:S(2)}, u32[]{:S(2)}) collective-permute-start(bf16[640,3584]{1,0:T(8,128)(2,1)} %get-tuple-element.30.v), channel_id=1, source_target_pairs={{0,24},{8,0},{16,8},{24,16},{1,25},{9,1},{17,9},{25,17},{2,26},{10... | collective-permute-start | bytes 13762568 | tf_op jit(solution)/shard_map/ppermute | solution.py:28
  228.5 829.0 %collective-permute-start.1 = (bf16[1024,3584]{1,0:T(8,128)(2,1)}, bf16[1024,3584]{1,0:T(8,128)(2,1)}, u32[]{:S(2)}, u32[]{:S(2)}) collective-permute-start(bf16[1024,3584]{1,0:T(8,128)(2,1)} %get-tuple-element.26.m), channel_id=1, source_target_pairs={{0,16},{8,24},{16,0},{24,8},{1,17},{9,25},{17,1},{25,9},{2,18},{10... | collective-permute-start | bytes 22020104 | tf_op jit(solution)/shard_map/ppermute | solution.py:21
  228.5 831.8 %collective-permute-start = (bf16[1024,3584]{1,0:T(8,128)(2,1)}, bf16[1024,3584]{1,0:T(8,128)(2,1)}, u32[]{:S(2)}, u32[]{:S(2)}) collective-permute-start(bf16[1024,3584]{1,0:T(8,128)(2,1)} %bitcast.8), channel_id=1, source_target_pairs={{0,16},{8,24},{16,0},{24,8},{1,17},{9,25},{17,1},{25,9},{2,18},{10... | collective-permute-start | bytes 22020104 | tf_op jit(solution)/shard_map/ppermute | solution.py:21
  328.2 412.0 %collective-permute-start.4 = (bf16[640,3584]{1,0:T(8,128)(2,1)S(1)}, bf16[640,3584]{1,0:T(8,128)(2,1)}, u32[]{:S(2)}, u32[]{:S(2)}) collective-permute-start(bf16[640,3584]{1,0:T(8,128)(2,1)S(1)} %collective-permute-done.3), channel_id=1, source_target_pairs={{0,24},{8,0},{16,8},{24,16},{1,25},{9,1},{17,9},{25,17},{2,26},{10... | collective-permute-start | bytes 13762568 | tf_op jit(solution)/shard_map/ppermute | solution.py:28
  743.5 369.9 %collective-permute-start.5 = (bf16[128,3584]{1,0:T(8,128)(2,1)}, bf16[128,3584]{1,0:T(8,128)(2,1)S(1)}, u32[]{:S(2)}, u32[]{:S(2)}) collective-permute-start(bf16[128,3584]{1,0:T(8,128)(2,1)} %shard_map.78.v), channel_id=1, source_target_pairs={{0,16},{8,24},{16,0},{24,8},{1,17},{9,25},{17,1},{25,9},{2,18},{10... | collective-permute-start | bytes 2752520 | tf_op jit(solution)/shard_map/ppermute | solution.py:21
  1060.2 82.6 %collective-permute-start.2 = (bf16[96,3584]{1,0:T(8,128)(2,1)}, bf16[96,3584]{1,0:T(8,128)(2,1)S(1)}, u32[]{:S(2)}, u32[]{:S(2)}) collective-permute-start(bf16[96,3584]{1,0:T(8,128)(2,1)} %shard_map.77.v), channel_id=1, source_target_pairs={{0,16},{8,24},{16,0},{24,8},{1,17},{9,25},{17,1},{25,9},{2,18},{10... | collective-permute-start | bytes 2064392 | tf_op jit(solution)/shard_map/ppermute | solution.py:21
  1113.3 0.9 copy-start
  1117.1 50.3 %collective-permute-start.7 = (bf16[96,3584]{1,0:T(8,128)(2,1)}, bf16[96,3584]{1,0:T(8,128)(2,1)S(1)}, u32[]{:S(2)}, u32[]{:S(2)}) collective-permute-start(bf16[96,3584]{1,0:T(8,128)(2,1)} %shard_map.82.v), channel_id=1, source_target_pairs={{0,16},{8,24},{16,0},{24,8},{1,17},{9,25},{17,1},{25,9},{2,18},{10... | collective-permute-start | bytes 2064392 | tf_op jit(solution)/shard_map/ppermute | solution.py:21
  1142.8 0.9 copy-start.1
  1145.4 30.3 %collective-permute-start.6 = (bf16[64,3584]{1,0:T(8,128)(2,1)}, bf16[64,3584]{1,0:T(8,128)(2,1)S(1)}, u32[]{:S(2)}, u32[]{:S(2)}) collective-permute-start(bf16[64,3584]{1,0:T(8,128)(2,1)} %shard_map.81.v), channel_id=1, source_target_pairs={{0,16},{8,24},{16,0},{24,8},{1,17},{9,25},{17,1},{25,9},{2,18},{10... | collective-permute-start | bytes 1376264 | tf_op jit(solution)/shard_map/ppermute | solution.py:21
  1167.4 0.9 copy-start.2
  1175.8 0.8 copy-start.3

commit v5 on v2

--- a/solution.py
+++ b/solution.py
@@ -14,6 +14,7 @@
 FIX_TWO = 1.0 - 0.95**STEP
 TILE = 32
 BAND = 256
+PIECES = 4
 SHARES = (2, 4, 4, 4, 4, 4, 4, 3, 2, 1)
 
 
@@ -67,8 +68,14 @@
         )
     pl.semaphore_wait(barrier, 2 * parts)
 
-    send_old = remote(old, old2, old_send, old_recv, partner_at)
-    send_old.start()
+    size = rows // PIECES
+    pieces = [pl.ds(index * size, size) for index in range(PIECES)]
+    send_old = [
+        remote(old.at[piece], old2.at[piece], old_send.at[index], old_recv.at[index], partner_at)
+        for index, piece in enumerate(pieces)
+    ]
+    for copy in send_old:
+        copy.start()
     send_hop = remote(tok, place(half, slot), hop_send, hop_recv, other_at)
     came_hop = remote(tok, place(1 - half, slot), hop_send, hop_recv, other_at)
 
@@ -170,16 +177,23 @@
     total = jnp.sum(jnp.sum(total, axis=1, keepdims=True), axis=0, keepdims=True)
     clip = jnp.minimum(1.0, 1.0 / jnp.sqrt(total / (D * FF) + 1e-06))
 
-    @pl.loop(0, rows // 16)
-    def _(index):
-        high = pl.ds(pl.multiple_of(index * 16, 16), 16)
-        scaled = clip * grad[high, :]
-        first[high, :] = (0.9 * first[high, :].astype(jnp.float32) + 0.1 * scaled).astype(
-            jnp.bfloat16
+    send_first = []
+    for index, piece in enumerate(pieces):
+
+        @pl.loop(index * size // 16, (index + 1) * size // 16)
+        def _(step):
+            high = pl.ds(pl.multiple_of(step * 16, 16), 16)
+            scaled = clip * grad[high, :]
+            first[high, :] = (0.9 * first[high, :].astype(jnp.float32) + 0.1 * scaled).astype(
+                jnp.bfloat16
+            )
+
+        copy = remote(
+            first.at[piece], first2.at[piece], first_send.at[index], first_recv.at[index], partner_at
         )
-
-    send_first = remote(first, first2, first_send, first_recv, partner_at)
-    send_first.start()
+        copy.start()
+        send_first.append(copy)
+
     keeps = [pltpu.make_async_copy(first, first_out, local.at[0])]
     keeps[0].start()
 
@@ -200,8 +214,8 @@
         start += size
     for keep in keeps:
         keep.wait()
-    send_old.wait()
-    send_first.wait()
+    for copy in send_old + send_first:
+        copy.wait()
 
 
 def first_phase(tokens, upstream, weights, first_moment, second_moment, bit):
@@ -229,7 +243,9 @@
             pltpu.VMEM((8, BAND), jnp.float32),
             pltpu.VMEM((2 * parts, 8, BAND), jnp.float32),
         ]
-        + [dma(())] * 8
+        + [dma((PIECES,))] * 2
+        + [dma(())] * 4
+        + [dma((PIECES,))] * 2
         + [dma((parts - 1, 2)), dma((parts // 2, 2)), dma((2 * parts - 1,)), dma((2, wide))],
         cost_estimate=pl.CostEstimate(
             flops=4 * count * rows * cols, bytes_accessed=20 * rows * cols, transcendentals=0
@@ -265,7 +281,7 @@
     old = old.astype(jnp.float32)
     first = first.astype(jnp.float32)
     second = second.astype(jnp.float32)
-    update = first / FIX_ONE / (jnp.sqrt(second / FIX_TWO) + 1e-08)
+    update = first * (1.0 / FIX_ONE) / (jnp.sqrt(second * (1.0 / FIX_TWO)) + 1e-08)
     fresh = old - 0.05 * (update + 0.1 * old)
     return fresh.astype(jnp.bfloat16)
 

time: 960 us -> 960 us (level)
  no operation moved by 1% of the time
where the time goes in v5:
time: 960 us; the launch traced here: 959 us
  Pallas kernels  714 us (74%)
  waiting for transfers between devices  232 us (24%)
    pallas_call x1, Pallas kernels, first_phase(): pl.pallas_call(functools.partial(first_kernel, bit), in_specs=[anywhere]...  638 us
    ppermute x10, waiting for transfers between devices, partner(): return lax.ppermute(value, axis, pairs)  232 us
    pallas_call x10, Pallas kernels, mix_chunk(): pl.pallas_call(mix_kernel, grid=(rows // TILE,), in_specs=[far, far, far,...  53.6 us
    pallas_call x8, Pallas kernels, gate(): pl.pallas_call(gate_kernel, grid=(rows // TILE,), in_specs=[block] + [pl....  22.9 us
  transfers between devices with their start and end apart: 10, of which 10 were waited for; matrix products, arithmetic and copies ran while one was open for 0% of the time, Pallas kernels for 8%

profile of v5, /device:TPU:0, one launch (start us, length us, event | category | flops | bytes accessed | tf_op | source)
XLA Modules:
  0.0 958.9 jit_solution(11428343927609310097)
XLA Ops:
  0.6 637.6 %shard_map.76 = (bf16[1024,3584]{1,0:T(8,128)(2,1)}, bf16[1024,3584]{1,0:T(8,128)(2,1)}, bf16[1024,3584]{1,0:T(8,128)(2,1)}, bf16[64,3584]{1,0:T(8,128)(2,1)}, b...) custom-call(bf16[1024,512]{1,0:T(8,128)(2,1)} %bitcast.25, ...), custom_call_target="tpu_custom_call" | custom-call | flops 15032385536 | bytes 73400320 | tf_op jit(solution)/shard_map/pallas_call | solution.py:230
  638.2 0.1 collective-permute-start.1
  638.3 2.9 collective-permute-start
  641.2 38.8 %collective-permute-done.1.v2.refs_0_ = bf16[64,3584]{1,0:T(8,128)(2,1)S(1)} collective-permute-done((bf16[64,3584]{1,0:T(8,128)(2,1)}, bf16[64,3584]{1,0:T(8,128)(2,1)S(1)}, u32[]{:S(2)}, u32[]{:S(2)}) %collective-permute-start.1) | collective-permute-done | bytes 458784 | tf_op jit(solution)/shard_map/ppermute | solution.py:24
  680.1 0.8 copy-done.7
  680.9 3.3 shard_map.79.v
  684.2 0.0 collective-permute-start.3
  684.2 3.8 shard_map.77
  688.0 31.4 %collective-permute-done.refs_0_.v2 = bf16[128,3584]{1,0:T(8,128)(2,1)S(1)} collective-permute-done((bf16[128,3584]{1,0:T(8,128)(2,1)}, bf16[128,3584]{1,0:T(8,128)(2,1)S(1)}, u32[]{:S(2)}, u32[]{:S(2)}) %collective-permute-start) | collective-permute-done | bytes 917536 | tf_op jit(solution)/shard_map/ppermute | solution.py:24
  719.4 1.0 copy-done.5
  720.4 3.3 shard_map.78.v
  723.7 0.0 collective-permute-start.2
  723.7 6.3 shard_map.80
  730.0 28.7 %collective-permute-done.3.v2.refs_0_ = bf16[128,3584]{1,0:T(8,128)(2,1)S(1)} collective-permute-done((bf16[128,3584]{1,0:T(8,128)(2,1)}, bf16[128,3584]{1,0:T(8,128)(2,1)S(1)}, u32[]{:S(2)}, u32[]{:S(2)}) %collective-permute-start.3) | collective-permute-done | bytes 917536 | tf_op jit(solution)/shard_map/ppermute | solution.py:24
  758.7 0.9 copy-done.4
  759.6 3.4 shard_map.83.v
  763.0 0.0 collective-permute-start.5
  763.0 6.3 shard_map.81
  769.3 28.8 %collective-permute-done.2.refs_0_.v2 = bf16[128,3584]{1,0:T(8,128)(2,1)S(1)} collective-permute-done((bf16[128,3584]{1,0:T(8,128)(2,1)}, bf16[128,3584]{1,0:T(8,128)(2,1)S(1)}, u32[]{:S(2)}, u32[]{:S(2)}) %collective-permute-start.2) | collective-permute-done | bytes 917536 | tf_op jit(solution)/shard_map/ppermute | solution.py:24
  798.1 0.9 copy-done.2
  799.0 3.3 shard_map.82.v
  802.3 0.0 collective-permute-start.4
  802.3 6.3 shard_map.84
  808.6 28.8 %collective-permute-done.5.v2.refs_0_ = bf16[128,3584]{1,0:T(8,128)(2,1)S(1)} collective-permute-done((bf16[128,3584]{1,0:T(8,128)(2,1)}, bf16[128,3584]{1,0:T(8,128)(2,1)S(1)}, u32[]{:S(2)}, u32[]{:S(2)}) %collective-permute-start.5) | collective-permute-done | bytes 917536 | tf_op jit(solution)/shard_map/ppermute | solution.py:24
  837.4 0.9 copy-done.3
  838.3 3.3 shard_map.87.v
  841.6 0.0 collective-permute-start.7
  841.6 6.3 shard_map.85
  847.9 28.8 %collective-permute-done.4.refs_0_.v2 = bf16[128,3584]{1,0:T(8,128)(2,1)S(1)} collective-permute-done((bf16[128,3584]{1,0:T(8,128)(2,1)}, bf16[128,3584]{1,0:T(8,128)(2,1)S(1)}, u32[]{:S(2)}, u32[]{:S(2)}) %collective-permute-start.4) | collective-permute-done | bytes 917536 | tf_op jit(solution)/shard_map/ppermute | solution.py:24
  876.7 0.9 copy-done
  877.6 2.8 shard_map.86.v
  880.4 0.0 collective-permute-start.6
  880.4 6.3 shard_map.88
  886.7 24.4 %collective-permute-done.7.v2.refs_0_ = bf16[128,3584]{1,0:T(8,128)(2,1)S(1)} collective-permute-done((bf16[128,3584]{1,0:T(8,128)(2,1)}, bf16[128,3584]{1,0:T(8,128)(2,1)S(1)}, u32[]{:S(2)}, u32[]{:S(2)}) %collective-permute-start.7) | collective-permute-done | bytes 917536 | tf_op jit(solution)/shard_map/ppermute | solution.py:24
  911.1 0.9 copy-done.1
  912.0 1.8 shard_map.91.v
  913.8 0.0 collective-permute-start.9
  913.8 6.3 shard_map.89
  920.1 15.6 %collective-permute-done.6.refs_0_.v2 = bf16[96,3584]{1,0:T(8,128)(2,1)S(1)} collective-permute-done((bf16[96,3584]{1,0:T(8,128)(2,1)}, bf16[96,3584]{1,0:T(8,128)(2,1)S(1)}, u32[]{:S(2)}, u32[]{:S(2)}) %collective-permute-start.6) | collective-permute-done | bytes 688160 | tf_op jit(solution)/shard_map/ppermute | solution.py:24
  935.7 0.9 copy-done.6
  936.5 1.6 shard_map.90.v
  938.2 5.4 shard_map.92
  943.6 6.8 collective-permute-done.9.v2
  950.4 0.8 copy-done.8
  951.2 3.8 shard_map.93
  955.0 0.3 collective-permute-done.8.v2
  955.3 0.7 copy-done.9
  956.0 2.9 shard_map.94
  (11 shorter events, 0.0 us)
Async XLA Ops:
  638.2 41.8 %collective-permute-start.1 = (bf16[64,3584]{1,0:T(8,128)(2,1)}, bf16[64,3584]{1,0:T(8,128)(2,1)S(1)}, u32[]{:S(2)}, u32[]{:S(2)}) collective-permute-start(bf16[64,3584]{1,0:T(8,128)(2,1)} %get-tuple-element.61.v), channel_id=1, source_target_pairs={{0,16},{8,24},{16,0},{24,8},{1,17},{9,25},{17,1},{25,9},{2,18},{10... | collective-permute-start | bytes 1376264 | tf_op jit(solution)/shard_map/ppermute | solution.py:24
  638.3 81.1 %collective-permute-start = (bf16[128,3584]{1,0:T(8,128)(2,1)}, bf16[128,3584]{1,0:T(8,128)(2,1)S(1)}, u32[]{:S(2)}, u32[]{:S(2)}) collective-permute-start(bf16[128,3584]{1,0:T(8,128)(2,1)} %get-tuple-element.60.v), channel_id=1, source_target_pairs={{0,16},{8,24},{16,0},{24,8},{1,17},{9,25},{17,1},{25,9},{2,18},{10... | collective-permute-start | bytes 2752520 | tf_op jit(solution)/shard_map/ppermute | solution.py:24
  680.1 0.8 copy-start.7
  684.2 74.5 %collective-permute-start.3 = (bf16[128,3584]{1,0:T(8,128)(2,1)}, bf16[128,3584]{1,0:T(8,128)(2,1)S(1)}, u32[]{:S(2)}, u32[]{:S(2)}) collective-permute-start(bf16[128,3584]{1,0:T(8,128)(2,1)} %shard_map.79.v), channel_id=1, source_target_pairs={{0,16},{8,24},{16,0},{24,8},{1,17},{9,25},{17,1},{25,9},{2,18},{10... | collective-permute-start | bytes 2752520 | tf_op jit(solution)/shard_map/ppermute | solution.py:24
  719.4 1.0 copy-start.5
  723.7 74.4 %collective-permute-start.2 = (bf16[128,3584]{1,0:T(8,128)(2,1)}, bf16[128,3584]{1,0:T(8,128)(2,1)S(1)}, u32[]{:S(2)}, u32[]{:S(2)}) collective-permute-start(bf16[128,3584]{1,0:T(8,128)(2,1)} %shard_map.78.v), channel_id=1, source_target_pairs={{0,16},{8,24},{16,0},{24,8},{1,17},{9,25},{17,1},{25,9},{2,18},{10... | collective-permute-start | bytes 2752520 | tf_op jit(solution)/shard_map/ppermute | solution.py:24
  758.7 0.9 copy-start.4
  763.0 74.4 %collective-permute-start.5 = (bf16[128,3584]{1,0:T(8,128)(2,1)}, bf16[128,3584]{1,0:T(8,128)(2,1)S(1)}, u32[]{:S(2)}, u32[]{:S(2)}) collective-permute-start(bf16[128,3584]{1,0:T(8,128)(2,1)} %shard_map.83.v), channel_id=1, source_target_pairs={{0,16},{8,24},{16,0},{24,8},{1,17},{9,25},{17,1},{25,9},{2,18},{10... | collective-permute-start | bytes 2752520 | tf_op jit(solution)/shard_map/ppermute | solution.py:24
  798.0 0.9 copy-start.2
  802.3 74.4 %collective-permute-start.4 = (bf16[128,3584]{1,0:T(8,128)(2,1)}, bf16[128,3584]{1,0:T(8,128)(2,1)S(1)}, u32[]{:S(2)}, u32[]{:S(2)}) collective-permute-start(bf16[128,3584]{1,0:T(8,128)(2,1)} %shard_map.82.v), channel_id=1, source_target_pairs={{0,16},{8,24},{16,0},{24,8},{1,17},{9,25},{17,1},{25,9},{2,18},{10... | collective-permute-start | bytes 2752520 | tf_op jit(solution)/shard_map/ppermute | solution.py:24
  837.4 0.9 copy-start.3
  841.6 69.5 %collective-permute-start.7 = (bf16[128,3584]{1,0:T(8,128)(2,1)}, bf16[128,3584]{1,0:T(8,128)(2,1)S(1)}, u32[]{:S(2)}, u32[]{:S(2)}) collective-permute-start(bf16[128,3584]{1,0:T(8,128)(2,1)} %shard_map.87.v), channel_id=1, source_target_pairs={{0,16},{8,24},{16,0},{24,8},{1,17},{9,25},{17,1},{25,9},{2,18},{10... | collective-permute-start | bytes 2752520 | tf_op jit(solution)/shard_map/ppermute | solution.py:24
  876.7 0.9 copy-start
  880.4 55.3 %collective-permute-start.6 = (bf16[96,3584]{1,0:T(8,128)(2,1)}, bf16[96,3584]{1,0:T(8,128)(2,1)S(1)}, u32[]{:S(2)}, u32[]{:S(2)}) collective-permute-start(bf16[96,3584]{1,0:T(8,128)(2,1)} %shard_map.86.v), channel_id=1, source_target_pairs={{0,16},{8,24},{16,0},{24,8},{1,17},{9,25},{17,1},{25,9},{2,18},{10... | collective-permute-start | bytes 2064392 | tf_op jit(solution)/shard_map/ppermute | solution.py:24
  911.1 0.9 copy-start.1
  913.8 36.6 %collective-permute-start.9 = (bf16[64,3584]{1,0:T(8,128)(2,1)}, bf16[64,3584]{1,0:T(8,128)(2,1)S(1)}, u32[]{:S(2)}, u32[]{:S(2)}) collective-permute-start(bf16[64,3584]{1,0:T(8,128)(2,1)} %shard_map.91.v), channel_id=1, source_target_pairs={{0,16},{8,24},{16,0},{24,8},{1,17},{9,25},{17,1},{25,9},{2,18},{10... | collective-permute-start | bytes 1376264 | tf_op jit(solution)/shard_map/ppermute | solution.py:24
  935.7 0.9 copy-start.6
  938.2 17.1 %collective-permute-start.8 = (bf16[32,3584]{1,0:T(8,128)(2,1)}, bf16[32,3584]{1,0:T(8,128)(2,1)S(1)}, u32[]{:S(2)}, u32[]{:S(2)}) collective-permute-start(bf16[32,3584]{1,0:T(8,128)(2,1)} %shard_map.90.v), channel_id=1, source_target_pairs={{0,16},{8,24},{16,0},{24,8},{1,17},{9,25},{17,1},{25,9},{2,18},{10... | collective-permute-start | bytes 688136 | tf_op jit(solution)/shard_map/ppermute | solution.py:24
  950.4 0.8 copy-start.8
  955.3 0.7 copy-start.9

commit v6 on v3

--- a/solution.py
+++ b/solution.py
@@ -12,7 +12,7 @@
 FIX_TWO = 1.0 - 0.95**STEP
 TILE = 32
 BAND = 256
-SHARES = (20, 4, 3, 3, 2)
+SHARES = (12, 5, 4, 4, 3, 2, 2)
 
 
 def partner(value, axis, bit):
@@ -255,7 +255,7 @@
     old = old.astype(jnp.float32)
     first = first.astype(jnp.float32)
     second = second.astype(jnp.float32)
-    update = first / FIX_ONE / (jnp.sqrt(second / FIX_TWO) + 1e-08)
+    update = first * (1.0 / FIX_ONE) / (jnp.sqrt(second * (1.0 / FIX_TWO)) + 1e-08)
     fresh = old - 0.05 * (update + 0.1 * old)
     return fresh.astype(jnp.bfloat16)
 
@@ -305,7 +305,7 @@
     first, chunks = first_phase(tokens[0], grad_out[0], first_moment[0], second_moment[0])
     first2 = partner(first, "replica", bit)
     arrived, mixed, outs, start = [], [], (), 0
-    waits = (weights2, 0, first2, 1, 2)
+    waits = (weights2, 0, first2, 1, 2, 3, 4)
     for index, second in enumerate(chunks):
         wait = waits[index]
         after = [arrived[wait] if isinstance(wait, int) else wait]

time: 962 us -> 964 us (level)
    ppermute x7 -> x9, waiting for transfers between devices: 656 us -> 651 us  [partner(): return lax.ppermute(value, axis, pairs)]
    pallas_call x5 -> x7, Pallas kernels: 47.1 us -> 49.7 us  [mix_chunk(): pl.pallas_call(mix_kernel, grid=(rows // TILE,), in_specs=[far, far, far,...]
    pallas_call x5 -> x7, Pallas kernels: 22.9 us -> 24.6 us  [gate(): pl.pallas_call(gate_kernel, grid=(rows // TILE,), in_specs=[block] + [pl....]
  transfers between devices with their start and end apart: 7 -> 9, of which waited for: 6 -> 8; matrix products, arithmetic and copies ran while one was open for 0% -> 0% of each run, Pallas kernels for 30% -> 30%
where the time goes in v6:
time: 964 us; the launch traced here: 962 us
  waiting for transfers between devices  651 us (68%)
  Pallas kernels  297 us (31%)
    ppermute x9, waiting for transfers between devices, partner(): return lax.ppermute(value, axis, pairs)  651 us
    pallas_call x1, Pallas kernels, first_phase(): pl.pallas_call(first_kernel, in_specs=[anywhere] * 4, out_specs=(anywhere...  222 us
    pallas_call x7, Pallas kernels, mix_chunk(): pl.pallas_call(mix_kernel, grid=(rows // TILE,), in_specs=[far, far, far,...  49.7 us
    pallas_call x7, Pallas kernels, gate(): pl.pallas_call(gate_kernel, grid=(rows // TILE,), in_specs=[block] + [pl....  24.6 us
  transfers between devices with their start and end apart: 9, of which 8 were waited for; matrix products, arithmetic and copies ran while one was open for 0% of the time, Pallas kernels for 30%

profile of v6, /device:TPU:0, one launch (start us, length us, event | category | flops | bytes accessed | tf_op | source)
XLA Modules:
  0.0 962.4 jit_solution(18179148263098247862)
XLA Ops:
  0.6 4.1 collective-permute-start
  4.7 222.5 %shard_map.76 = (bf16[1024,3584]{1,0:T(8,128)(2,1)}, bf16[384,3584]{1,0:T(8,128)(2,1)}, bf16[160,3584]{1,0:T(8,128)(2,1)}, bf16[128,3584]{1,0:T(8,128)(2,1)}, bf...) custom-call(bf16[1024,512]{1,0:T(8,128)(2,1)} %bitcast.22, ...), custom_call_target="tpu_custom_call" | custom-call | flops 15032385536 | bytes 73400320 | tf_op jit(solution)/shard_map/pallas_call | solution.py:206
  227.2 0.4 collective-permute-start.1
  227.6 250.8 %collective-permute-done.refs_0_.w2 = bf16[1024,3584]{1,0:T(8,128)(2,1)} collective-permute-done((bf16[1024,3584]{1,0:T(8,128)(2,1)}, bf16[1024,3584]{1,0:T(8,128)(2,1)}, u32[]{:S(2)}, u32[]{:S(2)}) %collective-permute-start) | collective-permute-done | bytes 7340064 | tf_op jit(solution)/shard_map/ppermute | solution.py:21
  478.5 7.8 shard_map.78.v
  486.2 0.0 collective-permute-start.3
  486.2 266.5 %collective-permute-done.3.refs_0_.v2 = bf16[384,3584]{1,0:T(8,128)(2,1)S(1)} collective-permute-done((bf16[384,3584]{1,0:T(8,128)(2,1)}, bf16[384,3584]{1,0:T(8,128)(2,1)S(1)}, u32[]{:S(2)}, u32[]{:S(2)}) %collective-permute-start.3) | collective-permute-done | bytes 2752544 | tf_op jit(solution)/shard_map/ppermute | solution.py:21
  752.8 0.0 copy-start
  752.8 1.5 copy-done
  754.3 3.9 shard_map.79.v
  758.2 0.0 collective-permute-start.4
  758.2 0.0 collective-permute-done.1.refs_0_.m2
  758.2 3.3 shard_map.77.v
  761.5 2.9 collective-permute-start.2
  764.4 16.2 %shard_map.80 = (bf16[1024,3584]{1,0:T(8,128)(2,1)}, bf16[1024,3584]{1,0:T(8,128)(2,1)}, bf16[1024,3584]{1,0:T(8,128)(2,1)}, f32[8,128]{1,0:T(8,128)}) custom-call(bf16[1024,3584]{1,0:T(8,128)(2,1)} %bitcast.9, bf16[1024,3584]{1,0:T(8,128)(2,1)} %collective-permute-done.refs_0_.w2, bf16[1024,3584]{1,0:T(8,128)(2,1)} %get-tuple-element.36.m, ...), custom_call_target="tpu_custom_call" | custom-call | flops 41287680 | bytes 24772608 | tf_op jit(solution)/shard_map/pallas_call | solution.py:284
  780.7 51.1 %collective-permute-done.4.v2.refs_0_ = bf16[160,3584]{1,0:T(8,128)(2,1)S(1)} collective-permute-done((bf16[160,3584]{1,0:T(8,128)(2,1)}, bf16[160,3584]{1,0:T(8,128)(2,1)S(1)}, u32[]{:S(2)}, u32[]{:S(2)}) %collective-permute-start.4) | collective-permute-done | bytes 1146912 | tf_op jit(solution)/shard_map/ppermute | solution.py:21
  831.7 0.0 copy-start.1
  831.7 1.0 copy-done.1
  832.8 3.3 shard_map.83.v
  836.1 0.0 collective-permute-start.6
  836.1 7.9 shard_map.81
  844.0 27.1 %collective-permute-done.2.refs_0_.v2 = bf16[128,3584]{1,0:T(8,128)(2,1)S(1)} collective-permute-done((bf16[128,3584]{1,0:T(8,128)(2,1)}, bf16[128,3584]{1,0:T(8,128)(2,1)S(1)}, u32[]{:S(2)}, u32[]{:S(2)}) %collective-permute-start.2) | collective-permute-done | bytes 917536 | tf_op jit(solution)/shard_map/ppermute | solution.py:21
  871.1 0.0 copy-start.3
  871.1 0.9 copy-done.3
  872.0 2.8 shard_map.82.v
  874.8 0.0 collective-permute-start.5
  874.8 6.3 shard_map.84
  881.1 24.4 %collective-permute-done.6.v2.refs_0_ = bf16[128,3584]{1,0:T(8,128)(2,1)S(1)} collective-permute-done((bf16[128,3584]{1,0:T(8,128)(2,1)}, bf16[128,3584]{1,0:T(8,128)(2,1)S(1)}, u32[]{:S(2)}, u32[]{:S(2)}) %collective-permute-start.6) | collective-permute-done | bytes 917536 | tf_op jit(solution)/shard_map/ppermute | solution.py:21
  905.5 0.0 copy-start.2
  905.5 0.9 copy-done.2
  906.4 1.8 shard_map.87.v
  908.2 0.0 collective-permute-start.8
  908.2 6.3 shard_map.85
  914.5 15.6 %collective-permute-done.5.refs_0_.v2 = bf16[96,3584]{1,0:T(8,128)(2,1)S(1)} collective-permute-done((bf16[96,3584]{1,0:T(8,128)(2,1)}, bf16[96,3584]{1,0:T(8,128)(2,1)S(1)}, u32[]{:S(2)}, u32[]{:S(2)}) %collective-permute-start.5) | collective-permute-done | bytes 688160 | tf_op jit(solution)/shard_map/ppermute | solution.py:21
  930.1 0.0 copy-start.4
  930.1 0.9 copy-done.4
  930.9 1.8 shard_map.86.v
  932.7 0.0 collective-permute-start.7
  932.7 5.4 shard_map.88
  938.1 11.6 %collective-permute-done.8.v2 = bf16[64,3584]{1,0:T(8,128)(2,1)S(1)} collective-permute-done((bf16[64,3584]{1,0:T(8,128)(2,1)}, bf16[64,3584]{1,0:T(8,128)(2,1)S(1)}, u32[]{:S(2)}, u32[]{:S(2)}) %collective-permute-start.8) | collective-permute-done | bytes 458784 | tf_op jit(solution)/shard_map/ppermute | solution.py:21
  949.7 0.0 copy-start.5
  949.7 0.8 copy-done.5
  950.5 3.8 shard_map.89
  954.3 3.5 collective-permute-done.7.v2
  957.8 0.0 copy-start.6
  957.8 0.8 copy-done.6
  958.6 3.8 shard_map.90
Async XLA Ops:
  0.6 477.8 %collective-permute-start = (bf16[1024,3584]{1,0:T(8,128)(2,1)}, bf16[1024,3584]{1,0:T(8,128)(2,1)}, u32[]{:S(2)}, u32[]{:S(2)}) collective-permute-start(bf16[1024,3584]{1,0:T(8,128)(2,1)} %bitcast.8), channel_id=1, source_target_pairs={{0,16},{8,24},{16,0},{24,8},{1,17},{9,25},{17,1},{25,9},{2,18},{10... | collective-permute-start | bytes 22020104 | tf_op jit(solution)/shard_map/ppermute | solution.py:21
  227.2 531.0 %collective-permute-start.1 = (bf16[1024,3584]{1,0:T(8,128)(2,1)}, bf16[1024,3584]{1,0:T(8,128)(2,1)}, u32[]{:S(2)}, u32[]{:S(2)}) collective-permute-start(bf16[1024,3584]{1,0:T(8,128)(2,1)} %get-tuple-element.36.m), channel_id=1, source_target_pairs={{0,16},{8,24},{16,0},{24,8},{1,17},{9,25},{17,1},{25,9},{2,18},{10... | collective-permute-start | bytes 22020104 | tf_op jit(solution)/shard_map/ppermute | solution.py:21
  486.2 266.5 %collective-permute-start.3 = (bf16[384,3584]{1,0:T(8,128)(2,1)}, bf16[384,3584]{1,0:T(8,128)(2,1)S(1)}, u32[]{:S(2)}, u32[]{:S(2)}) collective-permute-start(bf16[384,3584]{1,0:T(8,128)(2,1)} %shard_map.78.v), channel_id=1, source_target_pairs={{0,16},{8,24},{16,0},{24,8},{1,17},{9,25},{17,1},{25,9},{2,18},{10... | collective-permute-start | bytes 8257544 | tf_op jit(solution)/shard_map/ppermute | solution.py:21
  752.8 1.5 copy-start
  758.2 73.5 %collective-permute-start.4 = (bf16[160,3584]{1,0:T(8,128)(2,1)}, bf16[160,3584]{1,0:T(8,128)(2,1)S(1)}, u32[]{:S(2)}, u32[]{:S(2)}) collective-permute-start(bf16[160,3584]{1,0:T(8,128)(2,1)} %shard_map.79.v), channel_id=1, source_target_pairs={{0,16},{8,24},{16,0},{24,8},{1,17},{9,25},{17,1},{25,9},{2,18},{10... | collective-permute-start | bytes 3440648 | tf_op jit(solution)/shard_map/ppermute | solution.py:21
  761.5 109.5 %collective-permute-start.2 = (bf16[128,3584]{1,0:T(8,128)(2,1)}, bf16[128,3584]{1,0:T(8,128)(2,1)S(1)}, u32[]{:S(2)}, u32[]{:S(2)}) collective-permute-start(bf16[128,3584]{1,0:T(8,128)(2,1)} %shard_map.77.v), channel_id=1, source_target_pairs={{0,16},{8,24},{16,0},{24,8},{1,17},{9,25},{17,1},{25,9},{2,18},{10... | collective-permute-start | bytes 2752520 | tf_op jit(solution)/shard_map/ppermute | solution.py:21
  831.7 1.0 copy-start.1
  836.1 69.4 %collective-permute-start.6 = (bf16[128,3584]{1,0:T(8,128)(2,1)}, bf16[128,3584]{1,0:T(8,128)(2,1)S(1)}, u32[]{:S(2)}, u32[]{:S(2)}) collective-permute-start(bf16[128,3584]{1,0:T(8,128)(2,1)} %shard_map.83.v), channel_id=1, source_target_pairs={{0,16},{8,24},{16,0},{24,8},{1,17},{9,25},{17,1},{25,9},{2,18},{10... | collective-permute-start | bytes 2752520 | tf_op jit(solution)/shard_map/ppermute | solution.py:21
  871.1 0.9 copy-start.3
  874.8 55.2 %collective-permute-start.5 = (bf16[96,3584]{1,0:T(8,128)(2,1)}, bf16[96,3584]{1,0:T(8,128)(2,1)S(1)}, u32[]{:S(2)}, u32[]{:S(2)}) collective-permute-start(bf16[96,3584]{1,0:T(8,128)(2,1)} %shard_map.82.v), channel_id=1, source_target_pairs={{0,16},{8,24},{16,0},{24,8},{1,17},{9,25},{17,1},{25,9},{2,18},{10... | collective-permute-start | bytes 2064392 | tf_op jit(solution)/shard_map/ppermute | solution.py:21
  905.5 0.9 copy-start.2
  908.2 41.5 %collective-permute-start.8 = (bf16[64,3584]{1,0:T(8,128)(2,1)}, bf16[64,3584]{1,0:T(8,128)(2,1)S(1)}, u32[]{:S(2)}, u32[]{:S(2)}) collective-permute-start(bf16[64,3584]{1,0:T(8,128)(2,1)} %shard_map.87.v), channel_id=1, source_target_pairs={{0,16},{8,24},{16,0},{24,8},{1,17},{9,25},{17,1},{25,9},{2,18},{10... | collective-permute-start | bytes 1376264 | tf_op jit(solution)/shard_map/ppermute | solution.py:21
  930.1 0.9 copy-start.4
  932.7 25.1 %collective-permute-start.7 = (bf16[64,3584]{1,0:T(8,128)(2,1)}, bf16[64,3584]{1,0:T(8,128)(2,1)S(1)}, u32[]{:S(2)}, u32[]{:S(2)}) collective-permute-start(bf16[64,3584]{1,0:T(8,128)(2,1)} %shard_map.86.v), channel_id=1, source_target_pairs={{0,16},{8,24},{16,0},{24,8},{1,17},{9,25},{17,1},{25,9},{2,18},{10... | collective-permute-start | bytes 1376264 | tf_op jit(solution)/shard_map/ppermute | solution.py:21
  949.7 0.8 copy-start.5
  957.8 0.8 copy-start.6
